TPU v7x, 128 devices: a whole 4x4x4 slice. The times are simulated.
128 devices in a mesh: cuts: 64 (over z, y_hi, x, core), box: 2 (over y_lo).
Axes of the slice: x: 4, y: 4 (y_hi: 2, y_lo: 2; y = y_hi * 2 + y_lo), z: 4, core: 2. Of those that a mesh axis runs over, the one named last changes fastest.
Arguments:
- queries_in: bfloat16 [64, 8, 7, 256], P('cuts', 'box'), may hold values from -6 to 6
- image: bfloat16 [64, 4096, 256], P('cuts', 'box'), may hold values from -6 to 6
- box_coords: int32 [64, 8, 4], P('cuts', 'box'), may hold values from 0 to 1023
- box_mask: int32 [64, 8], P('cuts', 'box'), may hold values from 0 to 1, as said below
- volume_ids: int32 [64], P('cuts'), may hold values from 0 to 31, never falling along the last dimension, each value on 1 to 4 neighbouring positions
- cot_queries: bfloat16 [64, 8, 7, 256], P('cuts', 'box'), may hold values from -6 to 6
- cot_keys: bfloat16 [64, 8, 4096, 256], P('cuts', 'box'), may hold values from -6 to 6
- master: float32 [1579008], P(('cuts', 'box')), may hold values from -32 to 32, as said below
- moment1: float32 [1579008], P(('cuts', 'box')), may hold values from -16384 to 16384, as said below
- moment2: float32 [1579008], P(('cuts', 'box')), may hold values from 0 to 4194304, as said below
Outputs:
- queries_out: bfloat16 [64, 8, 7, 256], P('cuts', 'box')
- keys_out: bfloat16 [64, 8, 4096, 256], P('cuts', 'box')
- queries_grad: float32 [64, 8, 7, 256], P('cuts', 'box')
- image_grad: float32 [64, 4096, 256], P('cuts', 'box')
- new_master: float32 [1579008], P(('cuts', 'box'))
- new_first: float32 [1579008], P(('cuts', 'box'))
- new_second: float32 [1579008], P(('cuts', 'box'))
- new_copy: bfloat16 [1579008], P(('cuts', 'box'))
- matrix_norms: float32 [2, 14], replicated
Inputs may be any that keep to these rules, and one draw needn't show every extreme that they name: `box_mask`: every slice has at least two live boxes. `volume_ids`: volume numbers never fall from slice to slice; each volume has one to four slices. `master`: the parameters laid out as the first step states; padding entries are arbitrary. `moment1`: arbitrary real values. `moment2`: positive.
All inputs are finite; a program needn't handle non-finite values.
Results may differ from a plain program's by a relative error of at most 0.0018.
The roundings to bfloat16 on the way count: a program that leaves them out, or rounds other values in their place, can miss the bound.
Values may be sent and summed in bfloat16 or wider, within the bound.
No kernel may reach another device: no remote copies, remote signals or barrier semaphores. Data moves between devices by JAX's collectives and lax.ppermute only.
A program may use at most 256 MiB of HBM per device.

v0:
```python
import functools
import math

import jax
import jax.numpy as jnp
from jax import lax
from jax.sharding import Mesh
from jax.sharding import PartitionSpec as P

D = 256
INNER = 128
FF = 2048
HEADS = 8
GRID = 64
QT = 7
STEP = 5
CUTS = ("cuts_0", "cuts_1", "cuts_2", "cuts_3")
CUTS_BOX = ("cuts_0", "cuts_1", "cuts_2", "cuts_3", "box")


def over_axes(x, axes):
    return functools.reduce(lax.psum, axes, x)


def copy_for_each(x, axis):
    length = lax.axis_size(axis)
    return lax.all_to_all(jnp.broadcast_to(x[None], (length, *x.shape)), axis, 0, 0, tiled=True)


def laid_out(pieces, dim):
    dims = list(pieces.shape[1:])
    dims[dim] *= pieces.shape[0]
    return jnp.moveaxis(pieces, 0, dim).reshape(dims)


def collect(x, axis, dim):
    pieces = copy_for_each(x, axis)
    return laid_out(pieces, dim)


def in_blocks(x, dim, length):
    dims = x.shape
    pieces = x.reshape(*dims[:dim], length, dims[dim] // length, *dims[dim + 1 :])
    return jnp.moveaxis(pieces, dim, 0)


def sent_and_summed(x, axis, dim):
    pieces = in_blocks(x, dim, lax.axis_size(axis))
    arrived = lax.all_to_all(pieces, axis, split_axis=0, concat_axis=0, tiled=True)
    return arrived.sum(axis=0)


def piece_table(width, inner, hidden):
    table = [
        ("self_q", width, width, "matrix"),
        ("self_k", width, width, "matrix"),
        ("self_v", width, width, "matrix"),
        ("self_o", width, width, "matrix"),
        ("toimg_q", width, inner, "matrix"),
        ("toimg_k", width, inner, "matrix"),
        ("toimg_v", width, inner, "matrix"),
        ("toimg_o", inner, width, "matrix"),
        ("totok_q", width, inner, "matrix"),
        ("totok_k", width, inner, "matrix"),
        ("totok_v", width, inner, "matrix"),
        ("totok_o", inner, width, "matrix"),
        ("mlp_up", width, hidden, "matrix"),
        ("mlp_down", hidden, width, "matrix"),
        ("self_bq", 1, width, "bias"),
        ("self_bv", 1, width, "bias"),
        ("self_bo", 1, width, "bias"),
        ("toimg_bq", 1, inner, "bias"),
        ("toimg_bv", 1, inner, "bias"),
        ("toimg_bo", 1, width, "bias"),
        ("totok_bq", 1, inner, "bias"),
        ("totok_bv", 1, inner, "bias"),
        ("totok_bo", 1, width, "bias"),
        ("mlp_bup", 1, hidden, "bias"),
        ("mlp_bdown", 1, width, "bias"),
    ]
    for number in range(1, 5):
        table.append(("gain_" + str(number), 1, width, "gain"))
    for number in range(1, 5):
        table.append(("shift_" + str(number), 1, width, "bias"))
    return table


def unpack(flat, width, inner, hidden):
    found = {}
    offset = 0
    for name, rows, cols, kind in piece_table(width, inner, hidden):
        piece = flat[offset : offset + rows * cols]
        found[name] = piece.reshape(rows, cols) if kind == "matrix" else piece
        offset += rows * cols
    return found


def segment_members(positions, width, inner, hidden):
    columns = []
    offset = 0
    for name, rows, cols, kind in piece_table(width, inner, hidden):
        if kind == "matrix":
            columns.append((positions >= offset) & (positions < offset + rows * cols))
        offset += rows * cols
    return jnp.stack(columns, axis=1).astype(jnp.float32)


def product(left, right):
    return jnp.dot(left, right, precision=lax.Precision.HIGHEST, preferred_element_type=jnp.float32)


def fourier(across, down, width):
    order = jnp.arange(width // 2, dtype=jnp.float32)
    radius = 1.0 + jnp.mod(order, 4.0)
    turn = order * 2.39996
    phase = (
        2.0
        * math.pi
        * (across[..., None] * radius * jnp.cos(turn) + down[..., None] * radius * jnp.sin(turn))
    )
    return jnp.concatenate([jnp.sin(phase), jnp.cos(phase)], axis=-1)


def image_pe(grid, width):
    cells = jnp.arange(grid * grid, dtype=jnp.int32)
    across = 2.0 * ((cells % grid).astype(jnp.float32) + 0.5) / grid - 1.0
    down = 2.0 * ((cells // grid).astype(jnp.float32) + 0.5) / grid - 1.0
    return fourier(across, down, width)


def corner_pe(coords, tokens, width):
    points = (coords.astype(jnp.float32) + 0.5) / 1024.0 * 2.0 - 1.0
    first = fourier(points[..., 0], points[..., 1], width)
    second = fourier(points[..., 2], points[..., 3], width)
    blank = jnp.zeros(coords.shape[:-1] + (tokens - 2, width), jnp.float32)
    return jnp.concatenate([blank, first[..., None, :], second[..., None, :]], axis=-2)


def layer_norm(values, gain, shift):
    centered = values - jnp.mean(values, axis=-1, keepdims=True)
    spread = jnp.mean(centered * centered, axis=-1, keepdims=True)
    return centered * lax.rsqrt(spread + 1e-05) * gain + shift


def attend_heads(query, keyed, valued, w_out, b_out):
    inner = query.shape[1]
    size = inner // HEADS
    query = query.reshape(query.shape[0], HEADS, size) / math.sqrt(size)
    keyed = keyed.reshape(keyed.shape[0], HEADS, size)
    valued = valued.reshape(valued.shape[0], HEADS, size)
    if query.shape[0] >= keyed.shape[0]:
        scores = jnp.einsum("khe,qhe->hkq", keyed, query, precision=lax.Precision.HIGHEST)
        probs = jax.nn.softmax(scores, axis=1)
        mixed = jnp.einsum("hkq,khe->qhe", probs, valued, precision=lax.Precision.HIGHEST)
    else:
        scores = jnp.einsum("qhe,khe->hqk", query, keyed, precision=lax.Precision.HIGHEST)
        probs = jax.nn.softmax(scores, axis=2)
        mixed = jnp.einsum("hqk,khe->qhe", probs, valued, precision=lax.Precision.HIGHEST)
    return product(mixed.reshape(mixed.shape[0], inner), w_out) + b_out


def shared_side(flat, key_value, key_pe):
    parts = unpack(flat, D, INNER, FF)
    located = key_value + key_pe
    toimg_keys = product(located, parts["toimg_k"])
    toimg_values = product(key_value, parts["toimg_v"]) + parts["toimg_bv"]
    totok_query = product(located, parts["totok_q"]) + parts["totok_bq"]
    return (key_value, toimg_keys, toimg_values, totok_query)


def box_side(flat, shared, query_in, query_pe):
    parts = unpack(flat, D, INNER, FF)
    key_value, toimg_keys, toimg_values, totok_query = shared
    mixed_in = query_in + query_pe
    branch = attend_heads(
        product(mixed_in, parts["self_q"]) + parts["self_bq"],
        product(mixed_in, parts["self_k"]),
        product(query_in, parts["self_v"]) + parts["self_bv"],
        parts["self_o"],
        parts["self_bo"],
    )
    first = layer_norm(query_in + branch, parts["gain_1"], parts["shift_1"])
    branch = attend_heads(
        product(first + query_pe, parts["toimg_q"]) + parts["toimg_bq"],
        toimg_keys,
        toimg_values,
        parts["toimg_o"],
        parts["toimg_bo"],
    )
    second = layer_norm(first + branch, parts["gain_2"], parts["shift_2"])
    hidden = jax.nn.gelu(product(second, parts["mlp_up"]) + parts["mlp_bup"], approximate=False)
    third = layer_norm(
        second + product(hidden, parts["mlp_down"]) + parts["mlp_bdown"],
        parts["gain_3"],
        parts["shift_3"],
    )
    branch = attend_heads(
        totok_query,
        product(third + query_pe, parts["totok_k"]),
        product(third, parts["totok_v"]) + parts["totok_bv"],
        parts["totok_o"],
        parts["totok_bo"],
    )
    keys_out = layer_norm(key_value + branch, parts["gain_4"], parts["shift_4"])
    return (third, keys_out)


def local(
    queries_in,
    image,
    box_coords,
    box_mask,
    volume_ids,
    cot_queries,
    cot_keys,
    master,
    moment1,
    moment2,
):
    slices_here = queries_in.shape[0]
    volumes = slices_here * lax.axis_size(CUTS) // 2
    live = jnp.sum(box_mask, axis=1).astype(jnp.float32)
    belongs = (volume_ids[:, None] == jnp.arange(volumes, dtype=jnp.int32)[None, :]).astype(
        jnp.float32
    )
    count_term = jnp.sum(belongs * live[:, None], axis=0)
    shard_len = master.shape[0]
    positions = lax.axis_index(CUTS_BOX) * shard_len + jnp.arange(shard_len, dtype=jnp.int32)
    member = segment_members(positions, D, INNER, FF)
    weight_local = product(master * master, member)
    counts, weight_sq = (over_axes(count_term, CUTS_BOX), over_axes(weight_local, CUTS_BOX))
    flat = lax.all_gather(master.astype(jnp.bfloat16), CUTS_BOX, axis=0, tiled=True).astype(
        jnp.float32
    )
    scale = box_mask.astype(jnp.float32) / product(belongs, counts)[:, None]
    key_pe = image_pe(GRID, D)
    query_pe = corner_pe(box_coords, QT, D)

    def sweep(keys_whole):

        def per_slice(flat_grad, slice_inputs):
            key_rows, queries, pe_rows, cot_q, cot_k, weight_row = slice_inputs
            key_value = key_rows.astype(jnp.float32)
            shared, shared_back = jax.vjp(
                lambda params, keys: shared_side(params, keys, key_pe), flat, key_value
            )

            def per_box(inner_carry, box_inputs):
                total_grad, shared_cot = inner_carry
                query_rows, pe_one, cot_one_q, cot_one_k, weight_one = box_inputs

                def local_block(params, shared_value, query_value):
                    return box_side(params, shared_value, query_value, pe_one)

                outputs, pullback = jax.vjp(
                    local_block, flat, shared, query_rows.astype(jnp.float32)
                )
                grads = pullback(
                    (
                        cot_one_q.astype(jnp.float32) * weight_one,
                        cot_one_k.astype(jnp.float32) * weight_one,
                    )
                )
                summed = jax.tree.map(lambda left, right: left + right, shared_cot, grads[1])
                return (
                    (total_grad + grads[0], summed),
                    (outputs[0].astype(jnp.bfloat16), outputs[1].astype(jnp.bfloat16), grads[2]),
                )

            zero_shared = jax.tree.map(lambda value: jnp.zeros(value.shape, jnp.float32), shared)
            (total_grad, shared_cot), results = lax.scan(
                per_box, (flat_grad, zero_shared), (queries, pe_rows, cot_q, cot_k, weight_row)
            )
            param_part, key_grad = shared_back(shared_cot)
            total_grad = total_grad + param_part
            return (total_grad, (results, key_grad))

        flat_grad, (results, key_grads) = lax.scan(
            per_slice,
            jnp.zeros(flat.shape, jnp.float32),
            (keys_whole, queries_in, query_pe, cot_queries, cot_keys, scale),
        )
        return (flat_grad, results, key_grads)

    whole = collect(image, "box", 1)
    flat_grad, results, key_grads = sweep(whole)
    queries_out, keys_out, queries_grad = results
    image_grad = jax.tree.map(lambda part: sent_and_summed(part, "box", 1), key_grads)
    grad_shard = lax.psum_scatter(flat_grad, CUTS_BOX, scatter_dimension=0, tiled=True)
    new_first = 0.5 * moment1 + 0.5 * grad_shard
    new_second = 0.5 * moment2 + 0.5 * grad_shard * grad_shard
    fix = 1.0 - 0.5**STEP
    update = new_first / fix / (jnp.sqrt(new_second / fix) + 1e-06) + 0.01 * master
    update_local = product(update * update, member)
    update_sq = over_axes(update_local, CUTS_BOX)
    weight_norm = jnp.sqrt(weight_sq)
    update_norm = jnp.sqrt(update_sq)
    ratio = weight_norm / (update_norm + 1e-06)
    entry_ratio = product(member, ratio) + (1.0 - jnp.sum(member, axis=1))
    new_master = master - 0.25 * entry_ratio * update
    matrix_norms = jnp.stack([weight_norm, update_norm])
    return (
        queries_out,
        keys_out,
        queries_grad,
        image_grad,
        new_master,
        new_first,
        new_second,
        new_master.astype(jnp.bfloat16),
        matrix_norms,
    )


def solution(mesh):
    torus = Mesh(
        mesh.devices.reshape(4, 2, 4, 2, mesh.shape["box"]),
        ("cuts_0", "cuts_1", "cuts_2", "cuts_3", "box"),
    )
    in_specs = (
        P(CUTS, "box", None, None),
        P(CUTS, "box", None),
        P(CUTS, "box", None),
        P(CUTS, "box"),
        P(CUTS),
        P(CUTS, "box", None, None),
        P(CUTS, "box", None, None),
        P(CUTS_BOX),
        P(CUTS_BOX),
        P(CUTS_BOX),
    )
    out_specs = (
        P(CUTS, "box", None, None),
        P(CUTS, "box", None, None),
        P(CUTS, "box", None, None),
        P(CUTS, "box", None),
        P(CUTS_BOX),
        P(CUTS_BOX),
        P(CUTS_BOX),
        P(CUTS_BOX),
        P(),
    )
    return jax.shard_map(local, mesh=torus, in_specs=in_specs, out_specs=out_specs, check_vma=False)
```

profile of v0, /device:TPU:1, one launch (start us, length us, event | category | flops | bytes accessed | tf_op | source)
XLA Modules:
  0.0 1308.9 jit_solution(4437114956591009794)
XLA Ops:
  24.6 10.6 psum.105
  35.2 8.1 psum.106
  43.3 9.2 psum.107
  63.8 11.5 copy.129
  75.3 9.6 fusion.113
  100.6 77.2 %all-reduce.43.cloned.1.call-done = bf16[1579008]{0:T(1024)(128)(2,1)} async-done(((bf16[1579008]{0:T(1024)(128)(2,1)}), bf16[1579008]{0:T(1024)(128)(2,1)}) %all-reduce.43.cloned.1.call-update) | async-done | bytes 3158032
  198.2 873.2 %while.43 = (s32[]{:T(128)}, f32[1579008]{0:T(1024)}, f32[4096,256]{0,1:T(8,128)}, f32[4096,128]{0,1:T(8,128)}, f32[4096,128]{0,1:T(8,128)}, /*index=5*/f32[4096...) while((s32[]{:T(128)}, f32[1579008]{0:T(1024)}, ...), condition=%wide.region_49.50_spmd.clone, body=%wide.region_6.49_spmd.clone.sunk | while | flops 5822557184 | bytes 361649568 | solution.py:271
  239.5 7.7 fusion.452
  252.1 6.7 fusion.454
  373.3 35.2 %select_add_fusion.5 = f32[1579008]{0:T(1024)} fusion(f32[1579008]{0:T(1024)} %get-tuple-element.776, f32[65536]{0:T(1024)S(1)} %bitcast.538, f32[65536]{0:T(1024)S(1)} %bitcast.537, f32[65536]{0:T(1024)S(1)} %bitcast.536, f32[65536]{0:T(1024)S(1)} %bitcast.535, f32[32768]{0:T(1024)} %convolution_bitcast_fusion.52, f32[32768]{0:T(1024)} %bitcast.542, ...), kind=kLoop, calls=%fused_computation.3.clone.1 | loop fusion | flops 45791232 | bytes 18553856 | tf_op jit(solution)/shard_map/while/body/eval_jaxpr/while/body/eval_jaxpr/add | solution.py:266
  455.4 7.7 fusion.452
  589.8 35.7 %select_add_fusion.5 = f32[1579008]{0:T(1024)} fusion(f32[1579008]{0:T(1024)} %get-tuple-element.776, f32[65536]{0:T(1024)S(1)} %bitcast.538, f32[65536]{0:T(1024)S(1)} %bitcast.537, f32[65536]{0:T(1024)S(1)} %bitcast.536, f32[65536]{0:T(1024)S(1)} %bitcast.535, f32[32768]{0:T(1024)} %convolution_bitcast_fusion.52, f32[32768]{0:T(1024)} %bitcast.542, ...), kind=kLoop, calls=%fused_computation.3.clone.1 | loop fusion | flops 45791232 | bytes 18553856 | tf_op jit(solution)/shard_map/while/body/eval_jaxpr/while/body/eval_jaxpr/add | solution.py:266
  672.3 7.7 fusion.452
  806.7 35.7 %select_add_fusion.5 = f32[1579008]{0:T(1024)} fusion(f32[1579008]{0:T(1024)} %get-tuple-element.776, f32[65536]{0:T(1024)S(1)} %bitcast.538, f32[65536]{0:T(1024)S(1)} %bitcast.537, f32[65536]{0:T(1024)S(1)} %bitcast.536, f32[65536]{0:T(1024)S(1)} %bitcast.535, f32[32768]{0:T(1024)} %convolution_bitcast_fusion.52, f32[32768]{0:T(1024)} %bitcast.542, ...), kind=kLoop, calls=%fused_computation.3.clone.1 | loop fusion | flops 45791232 | bytes 18553856 | tf_op jit(solution)/shard_map/while/body/eval_jaxpr/while/body/eval_jaxpr/add | solution.py:266
  889.3 7.7 fusion.452
  1023.7 35.7 %select_add_fusion.5 = f32[1579008]{0:T(1024)} fusion(f32[1579008]{0:T(1024)} %get-tuple-element.776, f32[65536]{0:T(1024)S(1)} %bitcast.538, f32[65536]{0:T(1024)S(1)} %bitcast.537, f32[65536]{0:T(1024)S(1)} %bitcast.536, f32[65536]{0:T(1024)S(1)} %bitcast.535, f32[32768]{0:T(1024)} %convolution_bitcast_fusion.52, f32[32768]{0:T(1024)} %bitcast.542, ...), kind=kLoop, calls=%fused_computation.3.clone.1 | loop fusion | flops 45791232 | bytes 18553856 | tf_op jit(solution)/shard_map/while/body/eval_jaxpr/while/body/eval_jaxpr/add | solution.py:266
  1071.4 9.3 convolution_bitcast_fusion.20
  1085.5 9.2 convolution_bitcast_fusion.19
  1094.8 10.8 add_add_fusion.4
  1134.7 49.1 %all-to-all-done.1 = f32[2,1,2048,256]{3,2,1,0:T(8,128)} async-done(((f32[2,1,2048,256]{3,2,1,0:T(8,128)}), f32[2,1,2048,256]{3,2,1,0:T(8,128)}, u32[]{:S(2)}, u32[]{:S(2)}) %all-to-all-start.1) | async-done | bytes 4194336 | tf_op jit(solution)/shard_map/all_to_all | solution.py:49
  1187.9 77.0 %all-reduce.45.cloned.1.call-done = f32[1579008]{0:T(1024)} async-done(((f32[1579008]{0:T(1024)}), f32[1579008]{0:T(1024)}) %all-reduce.45.cloned.1.call-update) | async-done | bytes 6316048
  1267.1 8.5 all-reduce.36
  1280.9 7.0 all-reduce.35
  1287.9 8.4 all-reduce.38
  (1716 shorter events, 792.7 us)
Async XLA Ops:
  10.3 74.6 %all-to-all-start = ((bf16[2,1,2048,256]{2,3,1,0:T(8,128)(2,1)}), bf16[2,1,2048,256]{2,3,1,0:T(8,128)(2,1)}, u32[]{:S(2)}, u32[]{:S(2)}) async-start(bf16[2,1,2048,256]{2,3,1,0:T(8,128)(2,1)} %broadcast_in_dim.64), calls=%async_computation | async-start | bytes 4194304 | tf_op jit(solution)/shard_map/all_to_all | solution.py:27
  15.2 47.8 %copy-start.140 = (bf16[1,4,7,256]{3,1,2,0:T(4,128)(2,1)S(1)}, bf16[1,4,7,256]{3,1,2,0:T(4,128)(2,1)}, u32[]{:S(2)}) copy-start(bf16[1,4,7,256]{3,1,2,0:T(4,128)(2,1)} %param.12) | copy-start | bytes 43012
  15.2 47.8 %copy-start.141 = (bf16[1,4,7,256]{3,1,2,0:T(4,128)(2,1)S(1)}, bf16[1,4,7,256]{3,1,2,0:T(4,128)(2,1)}, u32[]{:S(2)}) copy-start(bf16[1,4,7,256]{3,1,2,0:T(4,128)(2,1)} %param.17) | copy-start | bytes 43012
  15.2 162.6 %all-reduce.43.cloned.1.call-start = ((), (), s32[]{:S(2)}) async-start(), calls=%async_computation.2 | async-start | bytes 6316032
  17.7 1247.2 %all-reduce.45.cloned.1.call-start = ((), (), s32[]{:S(2)}) async-start(), calls=%async_computation.3 | async-start | bytes 12632064
  87.7 108.3 %copy-start.22 = (bf16[2,1,2048,256]{3,2,0,1:T(8,128)(2,1)}, bf16[2,1,2048,256]{3,2,0,1:T(8,128)(2,1)S(1)}, u32[]{:S(2)}) copy-start(bf16[2,1,2048,256]{3,2,0,1:T(8,128)(2,1)S(1)} %copy.134) | copy-start | bytes 6291460
  199.8 33.5 %copy-start.68 = (f32[256]{0:T(256)}, f32[256]{0:T(256)S(1)}, u32[]{:S(2)}) copy-start(f32[256]{0:T(256)S(1)} %get-tuple-element.697) | copy-start | bytes 3076 | tf_op jit(solution)/shard_map/while/body/eval_jaxpr/while
  373.3 35.3 %copy-start.85 = (f32[7]{0:T(128)S(1)}, f32[7]{0:T(128)}, u32[]{:S(2)}) copy-start(f32[7]{0:T(128)} %copy-done.83) | copy-start | bytes 88 | tf_op jit(solution)/shard_map/while/body/eval_jaxpr/while
  373.3 35.3 %copy-start.91 = (f32[7]{0:T(128)S(1)}, f32[7]{0:T(128)}, u32[]{:S(2)}) copy-start(f32[7]{0:T(128)} %copy-done.89) | copy-start | bytes 88 | tf_op jit(solution)/shard_map/while/body/eval_jaxpr/while
  415.7 33.5 %copy-start.68 = (f32[256]{0:T(256)}, f32[256]{0:T(256)S(1)}, u32[]{:S(2)}) copy-start(f32[256]{0:T(256)S(1)} %get-tuple-element.697) | copy-start | bytes 3076 | tf_op jit(solution)/shard_map/while/body/eval_jaxpr/while
  589.8 35.8 %copy-start.85 = (f32[7]{0:T(128)S(1)}, f32[7]{0:T(128)}, u32[]{:S(2)}) copy-start(f32[7]{0:T(128)} %copy-done.83) | copy-start | bytes 88 | tf_op jit(solution)/shard_map/while/body/eval_jaxpr/while
  589.8 35.8 %copy-start.91 = (f32[7]{0:T(128)S(1)}, f32[7]{0:T(128)}, u32[]{:S(2)}) copy-start(f32[7]{0:T(128)} %copy-done.89) | copy-start | bytes 88 | tf_op jit(solution)/shard_map/while/body/eval_jaxpr/while
  632.7 33.5 %copy-start.68 = (f32[256]{0:T(256)}, f32[256]{0:T(256)S(1)}, u32[]{:S(2)}) copy-start(f32[256]{0:T(256)S(1)} %get-tuple-element.697) | copy-start | bytes 3076 | tf_op jit(solution)/shard_map/while/body/eval_jaxpr/while
  806.7 35.8 %copy-start.85 = (f32[7]{0:T(128)S(1)}, f32[7]{0:T(128)}, u32[]{:S(2)}) copy-start(f32[7]{0:T(128)} %copy-done.83) | copy-start | bytes 88 | tf_op jit(solution)/shard_map/while/body/eval_jaxpr/while
  806.7 35.8 %copy-start.91 = (f32[7]{0:T(128)S(1)}, f32[7]{0:T(128)}, u32[]{:S(2)}) copy-start(f32[7]{0:T(128)} %copy-done.89) | copy-start | bytes 88 | tf_op jit(solution)/shard_map/while/body/eval_jaxpr/while
  849.6 33.5 %copy-start.68 = (f32[256]{0:T(256)}, f32[256]{0:T(256)S(1)}, u32[]{:S(2)}) copy-start(f32[256]{0:T(256)S(1)} %get-tuple-element.697) | copy-start | bytes 3076 | tf_op jit(solution)/shard_map/while/body/eval_jaxpr/while
  1023.7 35.8 %copy-start.85 = (f32[7]{0:T(128)S(1)}, f32[7]{0:T(128)}, u32[]{:S(2)}) copy-start(f32[7]{0:T(128)} %copy-done.83) | copy-start | bytes 88 | tf_op jit(solution)/shard_map/while/body/eval_jaxpr/while
  1023.7 35.8 %copy-start.91 = (f32[7]{0:T(128)S(1)}, f32[7]{0:T(128)}, u32[]{:S(2)}) copy-start(f32[7]{0:T(128)} %copy-done.89) | copy-start | bytes 88 | tf_op jit(solution)/shard_map/while/body/eval_jaxpr/while
  1124.4 59.5 %all-to-all-start.1 = ((f32[2,1,2048,256]{3,2,1,0:T(8,128)}), f32[2,1,2048,256]{3,2,1,0:T(8,128)}, u32[]{:S(2)}, u32[]{:S(2)}) async-start(f32[2,1,2048,256]{3,2,1,0:T(8,128)} %bitcast.540), calls=%async_computation.1 | async-start | bytes 8388608 | tf_op jit(solution)/shard_map/all_to_all | solution.py:49
  1130.2 134.7 %copy-start.93 = (f32[12336]{0:T(1024)S(1)}, f32[12336]{0:T(1024)}, u32[]{:S(2)}) copy-start(f32[12336]{0:T(1024)} %param.19) | copy-start | bytes 148036
  1130.2 134.7 %copy-start.137 = (f32[12336]{0:T(1024)S(1)}, f32[12336]{0:T(1024)}, u32[]{:S(2)}) copy-start(f32[12336]{0:T(1024)} %param.20) | copy-start | bytes 148036
  1130.2 134.7 %copy-start.138 = (f32[12336]{0:T(1024)S(1)}, f32[12336]{0:T(1024)}, u32[]{:S(2)}) copy-start(f32[12336]{0:T(1024)} %param.21) | copy-start | bytes 148036
  1265.9 36.0 %copy-start.112 = (f32[12336]{0:T(1024)}, f32[12336]{0:T(1024)S(1)}, u32[]{:S(2)}) copy-start(f32[12336]{0:T(1024)S(1)} %get-tuple-element.373) | copy-start | bytes 148036
  1265.9 36.0 %copy-start.113 = (f32[12336]{0:T(1024)}, f32[12336]{0:T(1024)S(1)}, u32[]{:S(2)}) copy-start(f32[12336]{0:T(1024)S(1)} %get-tuple-element.374) | copy-start | bytes 148036
  (502 other events, 3759.0 us)
Sparse Core Ops, SparseCore 0:
  20.9 156.8 all-reduce.42
  1105.7 159.1 all-reduce.44
where the time goes:
time: 1330 us; the launch traced here: 1310 us
  matrix products  423 us (32%)
  other arithmetic  345 us (26%)
  local copies, waits for them, and re-layouts  227 us (17%)
  waiting for transfers between devices  203 us (15%)
  blocking collectives  69.5 us (5%)
  between operations  16.2 us (1%)
  loops' own time  14.4 us (1%)
    dot_general x144, matrix products, product(): jnp.dot(left, right, precision=lax.Precision.HIGHEST, preferred_element_t...  251 us
    unnamed x4, waiting for transfers between devices  154 us
    add x4, other arithmetic, per_box(): total_grad + grads[0]  142 us
    psum x10, blocking collectives, over_axes(): return functools.reduce(lax.psum, axes, x)  69.5 us
    slice x53, local copies, waits for them, and re-layouts, unpack(): piece = flat[offset:offset + rows * cols]  61 us
    all_to_all x1, waiting for transfers between devices, sent_and_summed(): lax.all_to_all(pieces, axis, split_axis=0, concat_axis=0, tiled=True)  49.1 us
    dot_general x12, matrix products, attend_heads(): jnp.einsum('hqk,khe->qhe', probs, valued, precision=lax.Precision.HIGHEST)  47.8 us
    dot_general x12, matrix products, attend_heads(): jnp.einsum('qhe,khe->hqk', query, keyed, precision=lax.Precision.HIGHEST)  42.9 us
  transfers between devices with their start and end apart: 4, of which 3 were waited for; matrix products, arithmetic and copies ran while one was open for 6% of the time, Pallas kernels for 0%

commit v1 on v0

v1 whole, which is shorter than its diff:
```python
import functools
import math

import jax
import jax.numpy as jnp
from jax import lax
from jax.experimental import pallas as pl
from jax.experimental.pallas import tpu as pltpu
from jax.sharding import Mesh
from jax.sharding import PartitionSpec as P

D = 256
INNER = 128
FF = 2048
HEADS = 8
GRID = 64
QT = 7
STEP = 5
CUTS = ("cuts_0", "cuts_1", "cuts_2", "cuts_3")
CUTS_BOX = ("cuts_0", "cuts_1", "cuts_2", "cuts_3", "box")
F32 = jnp.float32
BF = jnp.bfloat16
NEG = -1e30

MROWS = 12288
VLEN = 6144
VROWS = VLEN // 128
CHUNK = 112
PADDED = 12352
PEERS = 64
MATRIX_ROWS = (512, 512, 512, 512, 256, 256, 256, 256, 256, 256, 256, 256, 4096, 4096)
ROW0 = tuple(sum(MATRIX_ROWS[:i]) for i in range(15))
(SQ, SK, SV, SO, TQ, TK, TV, TO, UQ, UK, UV, UO, UP, DOWN) = ROW0[:14]
VECTORS = (
    ("s_bq", 256), ("s_bv", 256), ("s_bo", 256), ("t_bq", 128), ("t_bv", 128), ("t_bo", 256),
    ("u_bq", 128), ("u_bv", 128), ("u_bo", 256), ("bup", 2048), ("bdown", 256),
    ("g1", 256), ("g2", 256), ("g3", 256), ("g4", 256),
    ("h1", 256), ("h2", 256), ("h3", 256), ("h4", 256),
)
VOFF = {}
_at = 0
for _name, _len in VECTORS:
    VOFF[_name] = (_at, _len)
    _at += _len

TC = 512
IMG = GRID * GRID
STEPS = IMG // TC
HALF = STEPS // 2
TI = 1024
STEPS_I = IMG // TI
HALF_I = STEPS_I // 2
SENT = TC + 16 * (TC // 256)
RB = 64
SB = 64
PART0 = (0, 1, 2)
MIB = 1024 * 1024
MOST = 58 * MIB


def mm(a, b, ca=1, cb=0):
    return lax.dot_general(a, b, (((ca,), (cb,)), ((), ())), preferred_element_type=F32)


def split(x):
    hi = x.astype(BF)
    return hi, (x - hi.astype(F32)).astype(BF)


def mm_w(x, w, cb=0):
    hi, lo = split(x)
    rows = x.shape[0]
    y = mm(jnp.concatenate([hi, lo], axis=0), w, 1, cb)
    return y[:rows] + y[rows:]


def mm3(a, b, ca=1, cb=0):
    ah, al = split(a)
    bh, bl = split(b)
    return mm(ah, bh, ca, cb) + (mm(ah, bl, ca, cb) + mm(al, bh, ca, cb))


def mm3s(ah, al, bh, bl, ca=1, cb=0):
    return mm(ah, bh, ca, cb) + (mm(ah, bl, ca, cb) + mm(al, bh, ca, cb))


def cat3(a, dim):
    hi, lo = split(a)
    return jnp.concatenate([hi, hi, lo], axis=dim)


def cat3r(a, dim):
    hi, lo = split(a)
    return jnp.concatenate([hi, lo, hi], axis=dim)


def outer(a, b):
    ah, al = split(a)
    bh, bl = split(b)
    left = jnp.concatenate([ah, al, ah], axis=0)
    right = jnp.concatenate([bh, bh, bl], axis=0)
    return mm(left, right, 0, 0)


def iota(shape, dim):
    return lax.broadcasted_iota(jnp.int32, shape, dim)


def head_mask(width):
    c = iota((256, width), 0) % HEADS
    e = iota((256, width), 1) // (width // HEADS)
    return (c == e).astype(F32)


def expand(x, mask):
    n = x.shape[1]
    return jnp.broadcast_to(x[:, None, :], (32, HEADS, n)).reshape(256, n) * mask


def collapse(y, mask):
    n = y.shape[1]
    return jnp.sum((y * mask).reshape(32, HEADS, n), axis=1)


def live_rows(n):
    return (iota((32, n), 0) < 4 * QT).astype(F32)


def ln(x, gain, shift):
    centered = x - jnp.mean(x, axis=-1, keepdims=True)
    r = lax.rsqrt(jnp.mean(centered * centered, axis=-1, keepdims=True) + 1e-5)
    n = centered * r
    return n * gain + shift, n, r


def ln_back(dy, n, r, gain):
    h = dy * gain
    m1 = jnp.mean(h, axis=-1, keepdims=True)
    m2 = jnp.mean(h * n, axis=-1, keepdims=True)
    return r * (h - m1 - n * m2)


def col_sum(x):
    return jnp.sum(x, axis=0, keepdims=True)


def vget(ref, name):
    at, n = VOFF[name]
    row = at // 128
    return jnp.concatenate([ref[row + k : row + k + 1, :] for k in range(n // 128)], axis=1)


def wide(ref, row, n):
    left = ref[pl.ds(row, n, stride=2), :].astype(BF)
    right = ref[pl.ds(row + 1, n, stride=2), :].astype(BF)
    return jnp.concatenate([left, right], axis=1)


def pack256(ref, row, x):
    n = x.shape[0]
    ref[pl.ds(row, n, stride=2), :] = x[:, :128]
    ref[pl.ds(row + 1, n, stride=2), :] = x[:, 128:]


def chunk_row(p, core):
    device = (p // 2) * 4 + core * 2 + p % 2
    return pl.multiple_of(((771 * device) // 64) * 8, 8)


def fixed(x, dim=1):
    top = jnp.max(jnp.abs(x), axis=dim, keepdims=True)
    power = jnp.ceil(jnp.log2(jnp.maximum(top, 1e-30))) - 14.0
    return jnp.round(x * jnp.exp2(-power)).astype(jnp.int32), power


def on_lanes(column, rows):
    n = column.shape[0]
    return jnp.broadcast_to(column, (n, 128)).T[:rows]


def gelu_parts(x):
    cdf = 0.5 * (1.0 + lax.erf(x * math.sqrt(0.5)))
    return cdf


def in_vmem(n):
    return [pl.BlockSpec(memory_space=pltpu.VMEM)] * n


def specs(shapes):
    return [jax.ShapeDtypeStruct(shape, t) for shape, t, *_ in shapes]


def prep_kernel(half, sa, ca, sb, cb, *refs):
    k0_o, lh_o, ll_o, lht_o, llt_o, k0t_o = refs[-6:]
    k0 = half[...]
    rows = []
    for q in range(TC // GRID):
        s, c = sb[q : q + 1, :], cb[q : q + 1, :]
        rows.append(
            jnp.concatenate([sa[...] * c + ca[...] * s, ca[...] * c - sa[...] * s], axis=1)
        )
    loc = k0.astype(F32) + jnp.concatenate(rows, axis=0)
    hi, lo = split(loc)
    k0_o[...] = k0
    lh_o[...] = hi
    ll_o[...] = lo
    lht_o[...] = hi.T
    llt_o[...] = lo.T
    k0t_o[...] = k0.T


def prep(half, at, sa, ca, sb, cb, filled=()):
    col = pl.BlockSpec((D, TC), lambda j: (0, j + at))
    row = pl.BlockSpec((TC, D), lambda j: (j + at, 0))
    full = pl.BlockSpec((GRID, 128), lambda j: (0, 0))
    part = pl.BlockSpec((TC // GRID, 128), lambda j: (j + at, 0))
    rs = jax.ShapeDtypeStruct((IMG, D), BF)
    cs = jax.ShapeDtypeStruct((D, IMG), BF)
    return pl.pallas_call(
        prep_kernel,
        grid=(HALF,),
        in_specs=[pl.BlockSpec((TC, D), lambda j: (j, 0)), full, full, part, part]
        + [pl.BlockSpec(memory_space=pl.ANY)] * len(filled),
        out_specs=[row, row, row, col, col, col],
        out_shape=[rs, rs, rs, cs, cs, cs],
        input_output_aliases={5 + i: i for i in range(len(filled))},
        compiler_params=pltpu.CompilerParams(vmem_limit_bytes=MOST),
        cost_estimate=pl.CostEstimate(flops=10**9, bytes_accessed=8 * 10**6, transcendentals=0),
        name="prep",
    )(half, sa, ca, sb, cb, *filled)


HOPS = (0, -1, 1, 2)

STAT, SMALL, WT, TOK, TOK2, F1, U1, PRE, ROWS32 = 0, 16, 32, 64, 320, 448, 704, 960, 1216
NAR, NAR2, RR, VEC, PS, NARROW32 = 0, 32, 128, 224, 272, 528
SELF, TOW, UOW, UPB, DOWNB, ROWS16 = 0, 1024, 1152, 1280, 3328, 5376

G1, DM2, DF1, DPRE, DVW, DTOK, DNAR, DC2, DOTS, DGAIN, ROWSC = 0, 256, 512, 768, 1024, 1288, 1416, 1512, 1520, 1528, 1560


def tok32(ref, row, k):
    return ref[row + 32 * k : row + 32 * k + 32, :]


def up_blocks(w):
    return [w[UPB + 256 * k : UPB + 256 * k + 256, :] for k in range(8)]


def lay_weights(place, pieces, w_s, notes_s):
    core, y0 = place[1], place[2]
    w_s[...] = jnp.zeros((PADDED, 128), F32)
    keep = (iota((8, 128), 0) < 7).astype(F32)
    for at, n, copies, refs in pieces:
        for copy in copies:
            copy.wait()

        def lay(p, carry, refs=refs):
            k = p % 4
            y = (y0 + jnp.where(k == 1, 3, jnp.where(k == 2, 1, jnp.where(k == 3, 2, 0)))) % 4
            for ref, c, seen in zip(refs, (core, 1 - core), (0, PEERS)):
                device = (p // 16) * 32 + (y // 2) * 16 + ((p // 4) % 4) * 4 + c * 2 + y % 2
                row = ((771 * device) // 64) * 8
                block = ref[p].astype(F32)
                for lo, hi in ((0, 16), (16, 96), (96, CHUNK - 8), (CHUNK - 8, CHUNK)):
                    to = pl.ds(pl.multiple_of(row + lo, 8), hi - lo)
                    part = block[lo:hi]
                    if hi == CHUNK:
                        part = part * keep
                    w_s[to, :] = part if lo == 16 else w_s[to, :] + part
                notes_s[pl.ds(seen + p, 1), :] = block[CHUNK - 1 :, :]
            return carry

        lax.fori_loop(at, at + n, lay, 0, unroll=2)


def tokens_kernel(
    place, q0_i, pe_i, mine_h, other_h, lh_h, ll_h, k0t_h,
    s1_h, big_h, a32_h, b32_h, w16_h, slim_h,
    s1_o, big, a32, b32, w16, slim,
    w_s, notes_s, ut, mine_i, other_i, lh_i, ll_i, k0t_i, sems, sems_out,
):
    vec = b32.at[VEC : VEC + VROWS]
    leaving = []

    def leave(k, src, dst):
        copy = pltpu.make_async_copy(src, dst, sems_out.at[k])
        copy.start()
        leaving.append(copy)

    quarter = PEERS // 4
    pieces = []
    for k in range(4):
        part = pl.ds(k * quarter, quarter)
        copies = [
            pltpu.make_async_copy(src.at[part], dst.at[part], sems.at[2 * k + n])
            for n, (src, dst) in enumerate(((mine_h, mine_i), (other_h, other_i)))
        ]
        for copy in copies:
            copy.start()
        pieces.append((k * quarter, quarter, copies, (mine_i, other_i)))
    later = [
        pltpu.make_async_copy(src, dst, sems.at[8 + n])
        for n, (src, dst) in enumerate(((lh_h, lh_i), (ll_h, ll_i), (k0t_h, k0t_i)))
    ]
    for copy in later:
        copy.start()
    lay_weights(place, pieces, w_s, notes_s)
    notes = notes_s[...]
    same = notes[:, 4:5] == place[3].astype(F32)
    lane128 = iota((128, 128), 1)
    count = jnp.sum(col_sum(jnp.where(same & (lane128 < 4), notes, 0.0)), axis=1, keepdims=True)
    weights = [place[4 + b].astype(F32) / count for b in range(4)]
    a32[0:TOK, :] = jnp.zeros((TOK, 256), F32)
    for b in range(4):
        a32[WT + b : WT + b + 1, :] = jnp.broadcast_to(weights[b], (1, 256))
    vec[...] = w_s[MROWS : MROWS + VROWS, :]
    for k, at in enumerate((TQ, TK, TV, UQ, UK, UV)):
        slim[k] = w_s[at : at + 256, :].astype(BF)
    leave(0, slim, slim_h)
    for k, at in enumerate((SQ, SK, SV, SO)):
        w16[SELF + 256 * k : SELF + 256 * k + 256, :] = wide(w_s, at, 256)
    w16[TOW : TOW + 128, :] = wide(w_s, TO, 128)
    w16[UOW : UOW + 128, :] = wide(w_s, UO, 128)

    def self_w(k):
        return w16[SELF + 256 * k : SELF + 256 * k + 256, :]

    q0 = q0_i[...]
    pe = pe_i[...]
    m = q0 + pe
    q = mm_w(m, self_w(0)) + vget(vec, "s_bq")
    k = mm_w(m, self_w(1))
    v = mm_w(q0, self_w(2)) + vget(vec, "s_bv")
    m256 = head_mask(D)
    m128 = head_mask(INNER)
    qe = expand(q * (1.0 / math.sqrt(D // HEADS)), m256)
    s = mm3(qe, k, 1, 1)
    c = iota((256, 32), 0)
    r = iota((256, 32), 1)
    valid = ((c // HEADS) % 4 == r % 4) & (r < 4 * QT)
    s = jnp.where(valid, s, NEG)
    e = jnp.exp(s - jnp.max(s, axis=1, keepdims=True))
    p = e / jnp.sum(e, axis=1, keepdims=True)
    o = collapse(mm3(p, v), m256)
    a = mm_w(o, self_w(3)) + vget(vec, "s_bo")
    q1, n1, r1 = ln(q0 + a, vget(vec, "g1"), vget(vec, "h1"))
    qt = mm_w(q1 + pe, slim[0]) + vget(vec, "t_bq")
    qx = expand(qt * (1.0 / math.sqrt(INNER // HEADS)), m128)
    f1 = mm_w(qx, slim[1], 1)
    for at, x in enumerate((m, q0, q, k, v, o, n1, q1)):
        a32[TOK + 32 * at : TOK + 32 * at + 32, :] = x
    b32[NAR : NAR + 32, :] = qt
    b32[RR : RR + 32, :] = jnp.broadcast_to(r1, (32, 128))
    b32[PS : PS + 256, :] = jnp.concatenate([p, jnp.zeros((256, 96), F32)], axis=1)
    a32[F1 : F1 + 256, :] = f1
    f1t = cat3r(f1.T, 0)
    for copy in later:
        copy.wait()
    top = jnp.full((1, 256), NEG, F32)
    for j in range(STEPS_I):
        at = slice(j * TI, j * TI + TI)
        lh = lh_i[at, :]
        s1 = mm(jnp.concatenate([lh, lh, ll_i[at, :]], axis=1), f1t)
        s1_o[at, :] = s1
        top = jnp.maximum(top, jnp.max(s1, axis=0, keepdims=True))
    leave(1, s1_o, s1_h)
    total = jnp.zeros((1, 256), F32)
    for j in range(STEPS_I):
        at = slice(j * TI, j * TI + TI)
        e = jnp.exp(s1_o[at, :] - top)
        total = total + col_sum(e)
        eh, el = split(e)
        k0t = k0t_i[:, at]
        part = mm(jnp.concatenate([k0t, k0t], axis=1), jnp.concatenate([eh, el], axis=0))
        ut[...] = part if j == 0 else ut[...] + part
    for k in range(16):
        at = UPB + 256 * (k // 2)
        lanes = slice(128 * (k % 2), 128 * (k % 2) + 128)
        w16[at : at + 256, lanes] = w_s[pl.ds(UP + k, 256, stride=16), :].astype(BF)
    for k in range(8):
        w16[DOWNB + 256 * k : DOWNB + 256 * k + 256, :] = wide(w_s, DOWN + 512 * k, 256)
    leave(2, w16, w16_h)
    inverse = 1.0 / total
    a32[STAT : STAT + 1, :] = top
    a32[STAT + 1 : STAT + 2, :] = inverse
    u1 = (ut[...] * inverse).T
    a32[U1 : U1 + 256, :] = u1
    mixed = collapse(mm_w(u1, slim[2]), m128) + vget(vec, "t_bv")
    a = mm_w(mixed, w16[TOW : TOW + 128, :]) + vget(vec, "t_bo")
    q2, n2, r2 = ln(q1 + a, vget(vec, "g2"), vget(vec, "h2"))
    pre = jnp.concatenate([mm_w(q2, w) for w in up_blocks(w16)], axis=1) + vget(vec, "bup")
    for k in range(8):
        a32[PRE + 32 * k : PRE + 32 * k + 32, :] = pre[:, 256 * k : 256 * k + 256]
    hid = pre * gelu_parts(pre)
    y = mm_w(hid, w16[DOWNB : DOWNB + FF, :]) + vget(vec, "bdown")
    q3, n3, r3 = ln(q2 + y, vget(vec, "g3"), vget(vec, "h3"))
    live = live_rows(INNER)
    k2 = mm_w(q3 + pe, slim[4]) * live
    v2 = (mm_w(q3, slim[5]) + vget(vec, "u_bv")) * live
    for at, x in enumerate((n2, q2, n3, q3)):
        a32[TOK2 + 32 * at : TOK2 + 32 * at + 32, :] = x
    leave(6, a32.at[TOK:ROWS32], a32_h.at[TOK:ROWS32])
    for at, x in enumerate((mixed, k2, v2)):
        b32[NAR2 + 32 * at : NAR2 + 32 * at + 32, :] = x
    b32[RR + 32 : RR + 64, :] = jnp.broadcast_to(r2, (32, 128))
    b32[RR + 64 : RR + 96, :] = jnp.broadcast_to(r3, (32, 128))
    leave(3, b32, b32_h)
    kx = expand(k2 * (1.0 / math.sqrt(INNER // HEADS)), m128)
    m2 = mm_w(kx, slim[3], 1)
    c2 = mm3(jnp.broadcast_to(vget(vec, "u_bq"), (8, INNER)), kx, 1, 1)[0:1, :]
    lane = iota((1, 256), 1)
    a32[SMALL : SMALL + 8, :] = jnp.broadcast_to(jnp.where(lane >= 224, NEG, c2), (8, 256))
    rows = iota((256, 1), 0)
    spare = (rows >= 224) & (rows % 8 == 0)
    big[0:768, :] = cat3r(jnp.where(spare, -1.0, m2), 0)
    big[768:1536, :] = cat3r(m2.T, 0)
    leave(7, big.at[0:BIG_W], big_h.at[0:BIG_W])
    vw = mm_w(expand(v2, m128), w16[UOW : UOW + 128, :])
    wc = vw - jnp.mean(vw, axis=1, keepdims=True)
    bo = vget(vec, "u_bo")
    bo = bo - jnp.mean(bo, axis=1, keepdims=True)
    wfull = jnp.where(spare, bo, wc)
    wh = wfull.astype(BF).astype(F32)
    wl = wfull - wh
    rolled = jnp.concatenate([wh[248:], wh[:248]], axis=0)
    low = jnp.concatenate([wl[240:], wl[:240]], axis=0)
    cls = (rows // 8) % 4
    wt = wc.T
    lane_cls = (lane // 8) % 4
    wth = wt.astype(BF).astype(F32)
    wtl = pltpu.roll(wt - wth, 8, 1)
    gain = vget(vec, "g4")
    gain_col = jnp.broadcast_to(gain, (8, 256)).T[:, 0:1]
    row_o = a32.at[SMALL + 8 : SMALL + 16]
    for b in range(4):
        ws = jnp.where(
            cls == b, wh, jnp.where(cls == (b + 1) % 4, rolled, jnp.where(cls == (b + 2) % 4, low, 0.0))
        )
        big[BIG_W + 256 * b : BIG_W + 256 * b + 256, :] = ws.astype(BF)
        scaled = gain_col * weights[b]
        a = jnp.where(lane == 224 + 8 * b, scaled * (1.0 / D), wt * scaled)
        ah = a.astype(BF).astype(F32)
        al = pltpu.roll(a - ah, 8, 1)
        at = BIG_A + 1024 * (b % 2) + 512 * (b // 2)
        big[at : at + 256, :] = jnp.where(
            lane_cls == b, ah, jnp.where(lane_cls == (b + 1) % 4, al, 0.0)
        ).astype(BF)
        big[at + 256 : at + 512, :] = jnp.where(
            lane_cls == b, -wth, jnp.where(lane_cls == (b + 1) % 4, -wtl, 0.0)
        ).astype(BF)
        row_o[b : b + 1, :] = gain * weights[b]
    row_o[4:5, :] = gain
    row_o[5:6, :] = vget(vec, "h4")
    leave(4, big.at[BIG_W:BIG], big_h.at[BIG_W:BIG])
    leave(5, a32.at[0:TOK], a32_h.at[0:TOK])
    for copy in leaving:
        copy.wait()


BIG_W = 1536
BIG_A = BIG_W + 1024
BIG = BIG_A + 2048


def tokens(place, q0, pe, mine, other, lh, ll, k0t):
    out = [
        ((IMG, 256), F32),
        ((BIG, 256), BF),
        ((ROWS32, 256), F32),
        ((NARROW32, 128), F32),
        ((ROWS16, 256), BF),
        ((6, 256, 128), BF),
    ]
    return pl.pallas_call(
        tokens_kernel,
        in_specs=[pl.BlockSpec(memory_space=pltpu.SMEM)]
        + in_vmem(2)
        + [pl.BlockSpec(memory_space=pl.ANY)] * 5,
        out_specs=[pl.BlockSpec(memory_space=pl.ANY)] * len(out),
        out_shape=specs(out),
        scratch_shapes=[pltpu.VMEM(shape, t) for shape, t in out]
        + [
            pltpu.VMEM((PADDED, 128), F32),
            pltpu.VMEM((2 * PEERS, 128), F32),
            pltpu.VMEM((256, 256), F32),
            pltpu.VMEM((PEERS, CHUNK, 128), BF),
            pltpu.VMEM((PEERS, CHUNK, 128), BF),
            pltpu.VMEM((IMG, D), BF),
            pltpu.VMEM((IMG, D), BF),
            pltpu.VMEM((D, IMG), BF),
            pltpu.SemaphoreType.DMA((11,)),
            pltpu.SemaphoreType.DMA((len(out) + 2,)),
        ],
        compiler_params=pltpu.CompilerParams(vmem_limit_bytes=MOST),
        cost_estimate=pl.CostEstimate(flops=2 * 10**10, bytes_accessed=3 * 10**7, transcendentals=0),
        name="tokens",
    )(place, q0, pe, mine, other, lh, ll, k0t)


def group_max(x):
    m = jnp.maximum(x[:, :128], x[:, 128:])
    m = jnp.maximum(m, pltpu.roll(m, 64, 1))
    return jnp.maximum(m, pltpu.roll(m, 32, 1))


def group_sum(x):
    m = x[:, :128] + x[:, 128:]
    m = m + pltpu.roll(m, 64, 1)
    return m + pltpu.roll(m, 32, 1)


def twice(m):
    return jnp.concatenate([m, m], axis=1)


def image_kernel(
    place, cot_i, k0_i, lh_i, ll_i, lht_i, llt_i, s1_i, big_i, small_i, cq_i, *refs,
):
    late_refs, held, sems = refs[:4], refs[-5:-1], refs[-1]
    a32, b32, w16, slim = held
    later = [pltpu.make_async_copy(src, dst, sems.at[k]) for k, (src, dst) in enumerate(zip(late_refs, held))]
    image_steps(
        place, cot_i, k0_i, lh_i, ll_i, lht_i, llt_i, s1_i, big_i, small_i, cq_i, a32, b32, w16, slim, later, *refs[4:-5]
    )


def image_steps(
    place, cot_i, k0_i, lh_i, ll_i, lht_i, llt_i, s1_i, big_i, small_i, cq_i, a32, b32, w16, slim, later,
    keys_o, img_o, part0_o, part1_o, part2_o, c32,
    s_s, p_s, left_s, b_s, n_s, r_s, x_s, kc_s, acc, g2_o, dut, both,
):
    j = pl.program_id(0)

    @pl.when(j == 0)
    def _():
        for copy in later:
            copy.start()
        c32[...] = jnp.zeros((ROWSC, 256), F32)
        g2_o[...] = jnp.zeros(g2_o.shape, F32)

    @pl.when(j < STEPS_I)
    def _():
        image_part(
            cot_i, k0_i, lh_i, ll_i, lht_i, llt_i, big_i, small_i, keys_o,
            acc.at[pl.ds(pl.multiple_of(j * TI, TI), TI)], c32, g2_o,
            s_s, p_s, left_s, b_s, n_s, r_s, x_s, kc_s,
        )

    @pl.when(j == STEPS_I)
    def _():
        for copy in later:
            copy.wait()
        chain_part(cq_i, a32, b32, w16, slim, c32, g2_o, dut, both)

    def step(at, keep):
        image_step(
            s1_i, k0_i, lht_i, llt_i, acc.at[at * TI : at * TI + TI], a32, dut, both,
            c32.at[DOTS : DOTS + 8], c32.at[DF1 : DF1 + 256], keep,
        )

    def keep_send(refs, n, img):
        send(refs[n], img)

    def keep_own(n, img):
        img_o[n * TC : n * TC + TC, :] = img

    for n, refs in enumerate(((part0_o, part1_o), (part2_o.at[0:SENT], part2_o.at[SENT:]))):
        pl.when(j == STEPS_I + n)(functools.partial(step, HALF_I + n, functools.partial(keep_send, refs)))
    for n in range(HALF_I):
        pl.when(j == STEPS_I + HALF_I + n)(functools.partial(step, n, keep_own))


def image_part(
    cot_i, k0_i, lh_i, ll_i, lht_i, llt_i, big_i, small_i, keys_o, acc_o, c32, g2_o,
    s_s, p_s, left_s, b_s, n_s, r_s, x_s, kc_s,
):
    lh = lh_i[...]
    s_s[...] = mm(jnp.concatenate([lh, lh, ll_i[...]], axis=1), big_i[768:1536, :])
    lane = iota((SB, 256), 1)
    cls = (lane // 8) % 4
    for i in range(TI // SB):
        at = slice(i * SB, i * SB + SB)
        kf = k0_i[at, :].astype(F32)
        kc_s[at, :] = kf - jnp.mean(kf, axis=1, keepdims=True)
        s = s_s[at, :] + small_i[0:1, :]
        e = jnp.exp(s - twice(group_max(s)))
        p = e * twice(1.0 / group_sum(e))
        p = jnp.where((lane >= 224) & (lane % 8 == 0), 1.0, p)
        p_s[at, :] = p
        ph = p.astype(BF).astype(F32)
        plow = pltpu.roll(p - ph, 8, 1)
        pr = pltpu.roll(ph, 16, 1)
        for b in range(4):
            x = jnp.where(cls == b, ph, jnp.where(cls == (b + 1) % 4, plow, pr))
            left_s[b, at, :] = x.astype(BF)

    def product(b):
        b_s[b] = mm(left_s[b], big_i[BIG_W + 256 * b : BIG_W + 256 * b + 256, :])

    def box(b):
        for i in range(TI // RB):
            at = slice(i * RB, i * RB + RB)
            z = kc_s[at, :] + b_s[b, at, :]
            r = lax.rsqrt(jnp.mean(z * z, axis=1, keepdims=True) + 1e-5)
            n = z * r
            keys_o[b, at, :] = (n * small_i[12:13, :] + small_i[13:14, :]).astype(BF)
            g = cot_i[b, at, :].astype(F32)
            gn = g * n
            c32[DGAIN + 8 * b : DGAIN + 8 * b + 8, :] += jnp.sum(gn.reshape(RB // 8, 8, 256), axis=0)
            gain = small_i[8 + b : 9 + b, :]
            m2 = jnp.mean(gn * gain, axis=1, keepdims=True)
            nm = n * m2
            n_s[b, at, :] = nm.astype(BF)
            dz = r * (g * gain - nm)
            if b == 0:
                acc_o[at, :] = dz
            else:
                acc_o[at, :] += dz
            r_s[b, at, :] = jnp.broadcast_to(r, (RB, 128))

    def back_product(b):
        x_s[b] = mm(
            jnp.concatenate([cot_i[b], n_s[b], cot_i[b + 2], n_s[b + 2]], axis=1),
            big_i[BIG_A + 1024 * b : BIG_A + 1024 * b + 1024, :],
        )

    product(0)
    product(2)
    box(0)
    product(1)
    box(2)
    product(3)
    back_product(0)
    box(1)
    box(3)
    back_product(1)

    half = iota((SB, 128), 1)
    kind = (half // 8) % 4
    even = (lane // 8) % 2 == 0
    for i in range(TI // SB):
        at = slice(i * SB, i * SB + SB)
        rr = jnp.where(
            kind == 0,
            r_s[0, at, :],
            jnp.where(kind == 1, r_s[1, at, :], jnp.where(kind == 2, r_s[2, at, :], r_s[3, at, :])),
        )
        rr = twice(rr)
        xe = x_s[0, at, :]
        xo = x_s[1, at, :]
        x = jnp.where(even, xe, xo) + pltpu.roll(jnp.where(even, xo, xe), 248, 1)
        p = p_s[at, :]
        t = jnp.where(lane < 224, p, 0.0)
        dp = rr * x
        tdp = t * dp
        ds = tdp - t * twice(group_sum(tdp))
        s_s[at, :] = jnp.where((lane >= 224) & (lane % 8 == 0), dp, ds)
        p_s[at, :] = jnp.where((lane >= 224) & (lane % 8 == 1), 1.0, p * rr)

    ds = s_s[...]
    dh, dl = split(ds)
    acc_o[...] += mm(jnp.concatenate([dh, dh, dl], axis=1), big_i[0:768, :])
    lht = lht_i[...]
    c32[DM2 : DM2 + 256, :] += mm(
        jnp.concatenate([lht, llt_i[...], lht], axis=1), jnp.concatenate([dh, dh, dl], axis=0)
    )
    c32[DC2 : DC2 + 1, :] += col_sum(ds)
    l1 = p_s[...].T
    for b in range(4):
        pick = [l1[32 * i + 8 * b : 32 * i + 8 * b + 8] for i in range(8)]
        hi, lo = split(jnp.concatenate(pick, axis=0))
        y = mm(jnp.concatenate([hi, lo], axis=0), cot_i[b])
        c32[G1 + 64 * b : G1 + 64 * b + 64, :] += y[:64] + y[64:]
        g2_o[b] += mm(hi, n_s[b])


def image_side(place, cot, k0, lh, ll, lht, llt, s1, big, cq, a32, b32, w16, slim):
    def const(*shape):
        return pl.BlockSpec(shape, lambda j, place: (0,) * len(shape))

    def once(*shape):
        return pl.BlockSpec(shape, lambda j, place: (0,) * len(shape), pipeline_mode=pl.Buffered(1))

    def now(j):
        return jnp.minimum(j, STEPS_I - 1)

    def again(j):
        return jnp.where(j < STEPS_I, j, lax.rem(j + HALF_I, STEPS_I))

    row = pl.BlockSpec((TI, D), lambda j, place: (now(j), 0))
    row2 = pl.BlockSpec((TI, D), lambda j, place: (again(j), 0))
    col2 = pl.BlockSpec((D, TI), lambda j, place: (0, again(j)))
    late = pl.BlockSpec((TI, D), lambda j, place: (jnp.where(j < STEPS_I, HALF_I, again(j)), 0))
    boxes = pl.BlockSpec((4, TI, D), lambda j, place: (0, lax.rem(now(j) + place[0] * HALF_I, STEPS_I), 0))
    own = pl.BlockSpec((TI, D), lambda j, place: (jnp.maximum(j - STEPS_I - HALF_I, 0), 0))
    out = [
        ((4, IMG, D), BF, boxes),
        ((IMG // 2, D), F32, own),
        ((SENT, D), jnp.int16, None),
        ((SENT, D), jnp.int16, None),
        ((2 * SENT, D), jnp.int16, None),
        ((ROWSC, 256), F32, None),
    ]
    whole = [a32, b32, w16, slim]
    return pl.pallas_call(
        image_kernel,
        grid_spec=pltpu.PrefetchScalarGridSpec(
            num_scalar_prefetch=1,
            grid=(2 * STEPS_I,),
            in_specs=[boxes, row2, row, row, col2, col2, late, once(*big.shape)]
            + [pl.BlockSpec((16, 256), lambda j, place: (SMALL // 16, 0)), once(*cq.shape)]
            + [pl.BlockSpec(memory_space=pl.ANY)] * len(whole),
            out_specs=[s if s is not None else const(*shape) for shape, _, s in out],
            scratch_shapes=[
                pltpu.VMEM((TI, 256), F32),
                pltpu.VMEM((TI, 256), F32),
                pltpu.VMEM((4, TI, 256), BF),
                pltpu.VMEM((4, TI, 256), F32),
                pltpu.VMEM((4, TI, 256), BF),
                pltpu.VMEM((4, TI, 128), F32),
                pltpu.VMEM((2, TI, 256), F32),
                pltpu.VMEM((TI, 256), F32),
                pltpu.VMEM((IMG, 256), F32),
                pltpu.VMEM((4, 64, 256), F32),
                pltpu.VMEM((512, 256), BF),
                pltpu.VMEM((1536, 256), BF),
            ]
            + [pltpu.VMEM(x.shape, x.dtype) for x in whole]
            + [pltpu.SemaphoreType.DMA((len(whole),))],
        ),
        out_shape=specs(out),
        compiler_params=pltpu.CompilerParams(vmem_limit_bytes=MOST),
        cost_estimate=pl.CostEstimate(flops=5 * 10**10, bytes_accessed=4 * 10**7, transcendentals=0),
        name="image_side",
    )(place, cot, k0, lh, ll, lht, llt, s1, big, a32, cq, *whole)


def image_step(s1_i, k0_i, lht_i, llt_i, acc_i, stat_i, dut, both, dots, df1, keep):
    for n in range(TI // TC):
        at = slice(n * TC, n * TC + TC)
        k0 = k0_i[at, :]
        p = jnp.exp(s1_i[at, :] - stat_i[0:1, :]) * stat_i[1:2, :]
        dp = mm(jnp.concatenate([k0, k0], axis=1), dut[...])
        ds = p * (dp - dots[0:1, :])
        ph, plow = split(p)
        dh, dl = split(ds)
        img = acc_i[at, :] + mm(jnp.concatenate([ph, ph, plow, dh, dh, dl], axis=1), both[...])
        lht = lht_i[:, at]
        df1[...] += mm(
            jnp.concatenate([lht, llt_i[:, at], lht], axis=1), jnp.concatenate([dh, dh, dl], axis=0)
        )
        keep(n, img)


def send(ref, img):
    q, k = fixed(img)
    ref[0:TC, :] = q.astype(jnp.int16)
    k = on_lanes(k, 16).astype(jnp.int32).astype(jnp.int16)
    for part in range(TC // D):
        ref[TC + 16 * part : TC + 16 * part + 16, :] = k[:, D * part : D * part + D]


def chain_part(cq_i, a32, b32, w16, slim, c32, g2_i, dut, both):
    m128 = head_mask(INNER)
    scale1 = 1.0 / math.sqrt(INNER // HEADS)
    vec = b32.at[VEC : VEC + VROWS]
    per_box = []
    for b in range(4):
        gain = a32[SMALL + 8 + b : SMALL + 9 + b, :]
        x = c32[G1 + 64 * b : G1 + 64 * b + 64, :] * gain - g2_i[b]
        per_box.append(x - jnp.mean(x, axis=1, keepdims=True))
    bo_sum = sum(x[56:57] for x in per_box)
    zero = jnp.zeros((8, 256), F32)
    dvw = jnp.concatenate(
        [per_box[b][8 * i : 8 * i + 8] if i < QT else zero for i in range(8) for b in range(4)],
        axis=0,
    )
    c32[DVW : DVW + 256, :] = dvw
    c32[DVW + 256 : DVW + 264, :] = jnp.broadcast_to(bo_sum, (8, 256))
    dv2 = collapse(mm_w(dvw, w16[UOW : UOW + 128, :], 1), m128)
    dc2_8 = jnp.broadcast_to(c32[DC2 : DC2 + 1, :], (8, 256))
    dk2x = mm_w(c32[DM2 : DM2 + 256, :].T, slim[3]) + dc2_8.T[:, 0:1] * vget(vec, "u_bq")
    dk2 = collapse(dk2x, m128) * scale1 * live_rows(INNER)
    box = iota((32, 1), 0) % 4
    weight = sum(jnp.where(box == b, a32[WT + b : WT + b + 1, 0:1], 0.0) for b in range(4))
    dq3 = cq_i[...] * weight + mm_w(dv2, slim[5], 1) + mm_w(dk2, slim[4], 1)
    dx3 = ln_back(dq3, tok32(a32, TOK2, 2), b32[RR + 64 : RR + 96, 0:1], vget(vec, "g3"))
    pre = jnp.concatenate([tok32(a32, PRE, k) for k in range(8)], axis=1)
    slope = gelu_parts(pre) + pre * (jnp.exp(-0.5 * pre * pre) * (1.0 / math.sqrt(2.0 * math.pi)))
    dpre = mm_w(dx3, w16[DOWNB : DOWNB + FF, :], 1) * slope
    dq2 = dx3 + sum(
        mm_w(dpre[:, 256 * k : 256 * k + 256], w, 1) for k, w in enumerate(up_blocks(w16))
    )
    dx2 = ln_back(dq2, tok32(a32, TOK2, 0), b32[RR + 32 : RR + 64, 0:1], vget(vec, "g2"))
    dmixed = mm_w(dx2, w16[TOW : TOW + 128, :], 1)
    du = mm_w(expand(dmixed, m128), slim[2], 1)
    dots = jnp.sum(du * a32[U1 : U1 + 256, :], axis=1, keepdims=True)
    c32[DOTS : DOTS + 8, :] = jnp.broadcast_to(dots, (256, 128)).T[0:8, :]
    duh, dul = split(du.T)
    dut[...] = jnp.concatenate([duh, dul], axis=0)
    both[...] = jnp.concatenate([cat3r(du, 0), cat3r(a32[F1 : F1 + 256, :], 0)], axis=0)
    for at, x in enumerate((dv2, dk2, dmixed)):
        c32[DNAR + 32 * at : DNAR + 32 * at + 32, 0:128] = x
    for at, x in enumerate((dq3, dx3, dq2, dx2)):
        c32[DTOK + 32 * at : DTOK + 32 * at + 32, :] = x
    for k in range(8):
        c32[DPRE + 32 * k : DPRE + 32 * k + 32, :] = dpre[:, 256 * k : 256 * k + 256]


def land_kernel(img, part, out):
    k = jnp.concatenate([part[TC + 16 * i : TC + 16 * i + 1, :] for i in range(TC // D)], axis=1)
    scale = jnp.exp2(jnp.broadcast_to(k.astype(F32), (8, TC)).T[:, 0:1])
    out[...] = img[...] + part[0:TC, :].astype(F32) * scale


def land(img, part, at):
    row = pl.BlockSpec((TC, D), lambda j: (j + at, 0))
    return pl.pallas_call(
        land_kernel,
        grid=(part.shape[0] // SENT,),
        in_specs=[row, pl.BlockSpec((SENT, D), lambda j: (j, 0))],
        out_specs=row,
        out_shape=jax.ShapeDtypeStruct(img.shape, F32),
        input_output_aliases={0: 0},
        compiler_params=pltpu.CompilerParams(vmem_limit_bytes=6 * MIB),
        name="land",
    )(img, part)


def vputter(ref, row0):
    def vput(name, x):
        at, n = VOFF[name]
        for k in range(n // 128):
            row = MROWS - row0 + at // 128 + k
            ref[row : row + 1, :] = x[:, 128 * k : 128 * k + 128]

    return vput


def grads_kernel(
    place, pe_i, a32, b32, slim, c32, w16_h,
    mine_o, other_o, dq_o,
    gm_o, self_i, sem,
):
    weights = pltpu.make_async_copy(w16_h.at[SELF : SELF + 1024], self_i, sem)
    weights.start()
    vec = b32.at[VEC : VEC + VROWS]
    m128 = head_mask(INNER)
    scale1 = 1.0 / math.sqrt(INNER // HEADS)
    vput = vputter(gm_o, 0)
    gm_o[MROWS:, :] = jnp.zeros((PADDED - MROWS, 128), F32)
    pe = pe_i[...]
    dv2, dk2, dmixed = (tok32(c32, DNAR, k)[:, 0:128] for k in range(3))
    dq3, dx3, dq2, dx2 = (tok32(c32, DTOK, k) for k in range(4))
    n2, q2, n3, q3 = (tok32(a32, TOK2, k) for k in range(4))
    mixed, k2, v2 = (tok32(b32, NAR2, k) for k in range(3))
    vput("g3", col_sum(dq3 * n3))
    vput("h3", col_sum(dq3))
    vput("bdown", col_sum(dx3))
    for g in range(8):
        pre = tok32(a32, PRE, g)
        pack256(gm_o, DOWN + 512 * g, outer(pre * gelu_parts(pre), dx3))
    dpre = [tok32(c32, DPRE, g) for g in range(8)]
    vput("bup", col_sum(jnp.concatenate(dpre, axis=1)))
    for g in range(8):
        y = outer(q2, dpre[g])
        gm_o[pl.ds(UP + 2 * g, 256, stride=16), :] = y[:, :128]
        gm_o[pl.ds(UP + 2 * g + 1, 256, stride=16), :] = y[:, 128:]
    vput("g2", col_sum(dq2 * n2))
    vput("h2", col_sum(dq2))
    vput("u_bo", c32[DVW + 256 : DVW + 257, :])
    vput("h4", sum(c32[G1 + 64 * b + 57 : G1 + 64 * b + 58, :] * a32[WT + b : WT + b + 1, :] for b in range(4)))
    vput("g4", sum(col_sum(c32[DGAIN + 8 * b : DGAIN + 8 * b + 8, :]) * a32[WT + b : WT + b + 1, :] for b in range(4)))
    pack256(gm_o, UO, mm3(expand(v2, m128), c32[DVW : DVW + 256, :], 0, 0))
    k2x = expand(k2, m128)
    gm_o[UQ : UQ + 256, :] = mm3(c32[DM2 : DM2 + 256, :], k2x) * scale1
    vput("u_bq", mm3(jnp.broadcast_to(c32[DC2 : DC2 + 1, :], (8, 256)), k2x)[0:1] * scale1)
    gm_o[UK : UK + 256, :] = outer(q3 + pe, dk2)
    gm_o[UV : UV + 256, :] = outer(q3, dv2)
    vput("u_bv", col_sum(dv2))
    vput("t_bo", col_sum(dx2))
    pack256(gm_o, TO, outer(mixed, dx2))
    vput("t_bv", col_sum(dmixed))
    gm_o[TV : TV + 256, :] = mm3(a32[U1 : U1 + 256, :], expand(dmixed, m128), 0, 0)
    dft = c32[DF1 : DF1 + 256, :]
    gm_o[TK : TK + 256, :] = mm3(dft, expand(b32[NAR : NAR + 32, :], m128)) * scale1
    dqt = collapse(mm_w(dft.T, slim[1]), m128) * scale1 * live_rows(INNER)
    vput("t_bq", col_sum(dqt))
    m, q0, q, k, v, o, n1, q1 = (tok32(a32, TOK, i) for i in range(8))
    gm_o[TQ : TQ + 256, :] = outer(q1 + pe, dqt)
    dq1 = dx2 + mm_w(dqt, slim[0], 1)
    vput("g1", col_sum(dq1 * n1))
    vput("h1", col_sum(dq1))
    dx1 = ln_back(dq1, n1, b32[RR : RR + 32, 0:1], vget(vec, "g1"))
    m256 = head_mask(D)
    scale = 1.0 / math.sqrt(D // HEADS)
    weights.wait()
    vput("s_bo", col_sum(dx1))
    pack256(gm_o, SO, outer(o, dx1))
    do = expand(mm_w(dx1, self_i[768:1024, :], 1), m256)
    p = b32[PS : PS + 256, 0:32]
    dv = mm3(p, do, 0, 0)
    dp = mm3(do, v, 1, 1)
    ds = p * (dp - jnp.sum(p * dp, axis=1, keepdims=True))
    dq = collapse(mm3(ds, k), m256) * scale
    dk = mm3(ds, expand(q, m256), 0, 0) * scale
    vput("s_bq", col_sum(dq))
    vput("s_bv", col_sum(dv))
    pack256(gm_o, SQ, outer(m, dq))
    pack256(gm_o, SK, outer(m, dk))
    pack256(gm_o, SV, outer(q0, dv))
    dq_o[...] = dx1 + mm_w(dq, self_i[0:256, :], 1) + mm_w(dk, self_i[256:512, :], 1) + mm_w(dv, self_i[512:768, :], 1)
    core = place[1]

    def hand(p, carry):
        for ref, c in ((mine_o, core), (other_o, 1 - core)):
            ref[p] = gm_o[pl.ds(chunk_row(p, c), CHUNK), :]
        return carry

    lax.fori_loop(0, PEERS, hand, 0, unroll=2)


def param_grads(*args):
    return pl.pallas_call(
        grads_kernel,
        in_specs=[pl.BlockSpec(memory_space=pltpu.SMEM)]
        + in_vmem(len(args) - 2)
        + [pl.BlockSpec(memory_space=pl.ANY)],
        out_specs=in_vmem(3),
        scratch_shapes=[
            pltpu.VMEM((PADDED, 128), F32),
            pltpu.VMEM((1024, 256), BF),
            pltpu.SemaphoreType.DMA,
        ],
        out_shape=specs([((PEERS, CHUNK, 128), F32), ((PEERS, CHUNK, 128), F32), ((32, 256), F32)]),
        compiler_params=pltpu.CompilerParams(vmem_limit_bytes=12 * MIB),
        cost_estimate=pl.CostEstimate(flops=2 * 10**10, bytes_accessed=10**4, transcendentals=0),
        name="param_grads",
    )(*args)


def merged(x):
    row = iota((CHUNK, 128), 0)
    q, k = fixed(x, 0)
    return jnp.where(row == CHUNK - 1, k.astype(jnp.int32), q).astype(jnp.int16)


def merge_kernel(a, b, out):
    def some(p, carry):
        out[p] = merged(a[p] + b[p])
        return carry

    lax.fori_loop(0, PEERS, some, 0, unroll=4)


def merge(a, b):
    return pl.pallas_call(
        merge_kernel,
        in_specs=in_vmem(2),
        out_specs=in_vmem(1)[0],
        out_shape=jax.ShapeDtypeStruct((PEERS, CHUNK, 128), jnp.int16),
        compiler_params=pltpu.CompilerParams(vmem_limit_bytes=4 * MIB),
        name="merge",
    )(a, b)


def settle_kernel(where, came, m, one, two, one_o, two_o, up_o, sq_o):
    def some(i, total):
        for p in range(4):
            x = came[4 * i + p].astype(F32)
            total = total + x * jnp.exp2(x[CHUNK - 1 :, :])
        return total

    g = lax.fori_loop(0, PEERS // 4, some, jnp.zeros((CHUNK, 128), F32))
    master = m[...]
    first = 0.5 * one[...] + 0.5 * g
    second = 0.5 * two[...] + 0.5 * g * g
    fix = 1.0 - 0.5**STEP
    update = first / fix / (jnp.sqrt(second / fix) + 1e-06) + 0.01 * master
    one_o[...] = first
    two_o[...] = second
    up_o[...] = update
    at = iota((CHUNK, 128), 0) * 128 + iota((CHUNK, 128), 1)
    start, cut, end, piece = (where[k] for k in range(4))
    lane = iota((1, 128), 1)
    line = jnp.zeros((1, 128), F32)
    for k, x in enumerate((master, update)):
        sq = x * x
        for lo, hi, slot in ((start, cut, piece), (cut, end, piece + 1)):
            part = jnp.where((at >= lo) & (at < hi), sq, 0.0)
            part = jnp.sum(col_sum(part), axis=1, keepdims=True)
            line = line + jnp.where(lane == slot + 64 * k, part, 0.0)
    sq_o[...] = jnp.broadcast_to(line[None], (2 * PEERS, 1, 128))


def settle(where, came, m, one, two):
    chunk = jax.ShapeDtypeStruct((CHUNK, 128), F32)
    return pl.pallas_call(
        settle_kernel,
        in_specs=[pl.BlockSpec(memory_space=pltpu.SMEM)] + in_vmem(4),
        out_specs=in_vmem(4),
        out_shape=[chunk, chunk, chunk, jax.ShapeDtypeStruct((2 * PEERS, 1, 128), F32)],
        compiler_params=pltpu.CompilerParams(vmem_limit_bytes=4 * MIB),
        name="settle",
    )(where, came, m, one, two)


def rates():
    order = jnp.arange(D // 2, dtype=F32)
    radius = 1.0 + jnp.mod(order, 4.0)
    turn = order * 2.39996
    return 2.0 * math.pi * radius * jnp.cos(turn), 2.0 * math.pi * radius * jnp.sin(turn)


def token_pe(coords):
    along, down = rates()
    points = (coords.astype(F32) + 0.5) / 1024.0 * 2.0 - 1.0
    points = points.reshape(4, 2, 2)
    phase = points[..., 0:1] * along + points[..., 1:2] * down
    corner = jnp.concatenate([jnp.sin(phase), jnp.cos(phase)], axis=-1)
    corner = jnp.swapaxes(corner, 0, 1).reshape(8, D)
    return jnp.concatenate([jnp.zeros((20, D), F32), corner, jnp.zeros((4, D), F32)], axis=0)


def by_token(x):
    y = jnp.swapaxes(x, 0, 1).reshape(4 * QT, x.shape[-1])
    return jnp.concatenate([y, jnp.zeros((4, x.shape[-1]), y.dtype)], axis=0)


def by_box(x):
    return jnp.swapaxes(x[: 4 * QT].reshape(QT, 4, x.shape[-1]), 0, 1)


def device_work(place, own, peer, queries, coords, cot_q, cot_k, mine, swap):
    along, down = rates()
    cells = jnp.arange(GRID, dtype=F32)
    across = 2.0 * (cells + 0.5) / GRID - 1.0
    line = jnp.mod(jnp.arange(GRID, dtype=jnp.int32) + place[0] * (GRID // 2), GRID).astype(F32)
    below = 2.0 * (line + 0.5) / GRID - 1.0
    pa = across[:, None] * along[None, :]
    pb = below[:, None] * down[None, :]
    tables = (jnp.sin(pa), jnp.cos(pa), jnp.sin(pb), jnp.cos(pb))
    ready = prep(peer, HALF, *tables, filled=prep(own, 0, *tables))
    pe = token_pe(coords)
    q0 = by_token(queries.astype(F32))
    cq = by_token(cot_q.astype(F32))
    place, ready, pe, q0, cq, mine = lax.optimization_barrier((place, ready, pe, q0, cq, mine))
    k0, lh, ll, lht, llt, k0t = ready
    s1, big, a32, b32, w16, slim = tokens(place, q0, pe, mine, swap(mine), lh, ll, k0t)
    keys, img, one, two, three, c32 = image_side(
        place, cot_k, k0, lh, ll, lht, llt, s1, big, cq, a32, b32, w16, slim
    )
    parts = one, two, three
    gmine, gother, dq = param_grads(place, pe, a32, b32, slim, c32, w16)
    queries_out = a32[TOK2 + 96 : TOK2 + 128]
    return by_box(queries_out).astype(BF), keys, by_box(dq), img, parts, gmine, gother


SWAP = [(0, 1), (1, 0)]
HALFWAY = ("cuts_0", "cuts_1", "cuts_2", "box")
RING_Y = ("cuts_1", "box")


def passed(x, axis, step):
    return lax.ppermute(x, axis, [(i, (i + step) % 4) for i in range(4)])


def ring_all(x, axis):
    return [x, passed(x, axis, 1), passed(x, axis, -1), passed(x, axis, 2)]


def swap(x):
    return lax.ppermute(x, "cuts_3", SWAP)


def local(
    queries_in, image, box_coords, box_mask, volume_ids, cot_queries, cot_keys, master, moment1, moment2,
):
    box = lax.axis_index("box")
    me = lax.axis_index(CUTS_BOX)
    own = image[0]
    shard = master.shape[0]
    first_row = ((771 * me) // 64) * 8
    shift = shard * me - 128 * first_row
    peer = lax.ppermute(own, "box", SWAP)
    room = 1024
    long = jnp.concatenate(
        [jnp.zeros((room,), BF), master.astype(BF), jnp.zeros((CHUNK * 128 - shard,), BF)]
    )
    chunk = lax.dynamic_slice(long, (room - shift,), (CHUNK * 128,)).reshape(CHUNK, 128)
    last = jnp.concatenate([box_mask[0].astype(BF), volume_ids.astype(BF), jnp.zeros((123,), BF)])
    chunk = jnp.where(jnp.arange(CHUNK, dtype=jnp.int32)[:, None] == CHUNK - 1, last[None], chunk)
    column = jnp.stack(ring_all(chunk, RING_Y))
    plane = lax.all_to_all(
        jnp.broadcast_to(column[None], (PEERS // 4, 4, CHUNK, 128)), ("cuts_0", "cuts_2"), 0, 0, tiled=True
    )
    mine = plane.reshape(PEERS, CHUNK, 128)
    place = jnp.concatenate(
        [
            jnp.stack([box, lax.axis_index("cuts_3"), 2 * lax.axis_index("cuts_1") + box, volume_ids[0]]),
            box_mask[0],
        ]
    ).astype(jnp.int32)

    queries_out, keys_out, queries_grad, img, parts, gmine, gother = device_work(
        place, own, peer, queries_in[0], box_coords[0], cot_queries[0], cot_keys[0], mine, swap
    )
    one, two, three = parts
    one = lax.ppermute(one, "box", SWAP)
    gother, one, two = lax.optimization_barrier((gother, one, two))
    two = lax.ppermute(two, "box", SWAP)

    start = shard * me
    edges = jnp.array([128 * r for r in ROW0[1:]], jnp.int32)
    piece = jnp.sum((edges <= start).astype(jnp.int32))
    edge = functools.reduce(
        lambda e, r: jnp.where((128 * r > start) & (e > 128 * r), 128 * r, e), ROW0[1:], start + shard
    )
    cut = jnp.minimum(edge, start + shard) - start

    def laid(x):
        return lax.dynamic_update_slice(jnp.zeros((CHUNK * 128,), F32), x, (shift,)).reshape(CHUNK, 128)

    def taken(x):
        return lax.dynamic_slice(x.reshape(CHUNK * 128), (shift,), (shard,))

    states = [laid(x) for x in (master, moment1, moment2)]
    sent = merge(gmine, swap(gother))
    sent, two, img = lax.optimization_barrier((sent, two, img))
    came = lax.all_to_all(sent, HALFWAY, 0, 0, tiled=True)
    img = land(land(img, one, PART0[0]), two, PART0[1])
    where = jnp.stack([shift, shift + cut, shift + shard, piece]).astype(jnp.int32)
    came, three, img, states, where = lax.optimization_barrier((came, three, img, states, where))
    three = lax.ppermute(three, "box", SWAP)
    new_first, new_second, update, squares = settle(where, came, *states)
    squares = lax.all_to_all(squares, CUTS_BOX, 0, 0, tiled=True)
    new_first, new_second, update = taken(new_first), taken(new_second), taken(update)
    image_grad = land(img, three, PART0[2])
    squares, image_grad = lax.optimization_barrier((squares, image_grad))
    squares = jnp.sum(squares, axis=(0, 1))
    weight_norm = jnp.sqrt(squares[:14])
    update_norm = jnp.sqrt(squares[64:78])
    ratio = jnp.concatenate([weight_norm / (update_norm + 1e-06), jnp.ones((2,), F32)])
    entry = jnp.where(jnp.arange(shard, dtype=jnp.int32) < cut, ratio[piece], ratio[piece + 1])
    new_master = master - 0.25 * entry * update
    return (
        queries_out[None],
        keys_out[None],
        queries_grad[None],
        image_grad[None],
        new_master,
        new_first,
        new_second,
        new_master.astype(BF),
        jnp.stack([weight_norm, update_norm]),
    )


def solution(mesh):
    torus = Mesh(
        mesh.devices.reshape(4, 2, 4, 2, mesh.shape["box"]),
        ("cuts_0", "cuts_1", "cuts_2", "cuts_3", "box"),
    )
    in_specs = (
        P(CUTS, "box", None, None),
        P(CUTS, "box", None),
        P(CUTS, "box", None),
        P(CUTS, "box"),
        P(CUTS),
        P(CUTS, "box", None, None),
        P(CUTS, "box", None, None),
        P(CUTS_BOX),
        P(CUTS_BOX),
        P(CUTS_BOX),
    )
    out_specs = (
        P(CUTS, "box", None, None),
        P(CUTS, "box", None, None),
        P(CUTS, "box", None, None),
        P(CUTS, "box", None),
        P(CUTS_BOX),
        P(CUTS_BOX),
        P(CUTS_BOX),
        P(CUTS_BOX),
        P(),
    )
    return jax.shard_map(local, mesh=torus, in_specs=in_specs, out_specs=out_specs, check_vma=False)
```

time: 1330 us -> 188 us (0.14); the launches traced: 1310 us -> 187 us
  matrix products: 423 us -> 0 us
  other arithmetic: 345 us -> 9.04 us
  local copies, waits for them, and re-layouts: 227 us -> 15 us
  waiting for transfers between devices: 203 us -> 37.9 us
  Pallas kernels: 0 us -> 85.9 us
  blocking collectives: 69.5 us -> 0 us
  starting transfers between devices: 10.7 us -> 33.7 us
  loops' own time: 14.4 us -> 0 us
    dot_general x216 -> x0, matrix products: 423 us -> none  [the longest x144 251 us: product(): jnp.dot(left, right, precision=lax.Precision.HIGHEST, preferred_element_t...]
    add x19 -> x0, other arithmetic: 192 us -> none  [the longest x4 142 us: per_box(): total_grad + grads[0]]
    unnamed x4 -> x0, waiting for transfers between devices: 154 us -> none
    pallas_call x0 -> x10, Pallas kernels: none -> 85.9 us  [the longest x1 46.7 us: image_side(): pl.pallas_call(image_kernel, grid_spec=pltpu.PrefetchScalarGridSpec(num_s...]
    reduce_sum x53 -> x2, other arithmetic: 72.1 us -> 0.78 us  [the longest x1 0.63 us: local(): piece = jnp.sum((edges <= start).astype(jnp.int32))]
    psum x10 -> x0, blocking collectives: 69.5 us -> none  [over_axes(): return functools.reduce(lax.psum, axes, x)]
    slice x54 -> x2, local copies, waits for them, and re-layouts: 61.2 us -> 0.77 us  [the longest x1 0.76 us: by_box(): return jnp.swapaxes(x[:4 * QT].reshape(QT, 4, x.shape[-1]), 0, 1)]
    while x1026 -> x0, local copies, waits for them, and re-layouts: 46.7 us -> none
  transfers between devices with their start and end apart: 4 -> 12, of which waited for: 3 -> 7; matrix products, arithmetic and copies ran while one was open for 6% -> 7% of each run, Pallas kernels for 0% -> 13%
where the time goes in v1:
time: 188 us; the launch traced here: 187 us
  Pallas kernels  85.9 us (46%)
  waiting for transfers between devices  37.9 us (20%)
  starting transfers between devices  33.7 us (18%)
  local copies, waits for them, and re-layouts  15 us (8%)
  other arithmetic  9.04 us (5%)
  between operations  5.09 us (3%)
    pallas_call x1, Pallas kernels, image_side(): pl.pallas_call(image_kernel, grid_spec=pltpu.PrefetchScalarGridSpec(num_s...  46.7 us
    all_to_all x1, waiting for transfers between devices, local(): came = lax.all_to_all(sent, HALFWAY, 0, 0, tiled=True)  18.3 us
    pallas_call x1, Pallas kernels, tokens(): pl.pallas_call(tokens_kernel, in_specs=[pl.BlockSpec(memory_space=pltpu.S...  15.3 us
    pallas_call x2, Pallas kernels, prep(): pl.pallas_call(prep_kernel, grid=(HALF,), in_specs=[pl.BlockSpec((TC, D),...  8.88 us
    ppermute x2, waiting for transfers between devices, swap(): return lax.ppermute(x, 'cuts_3', SWAP)  7.97 us
    all_to_all x1, starting transfers between devices, local(): lax.all_to_all(jnp.broadcast_to(column[None], (PEERS // 4, 4, CHUNK, 128)...  7.73 us
    unnamed x38, local copies, waits for them, and re-layouts  6.68 us
    pallas_call x3, Pallas kernels, land(): pl.pallas_call(land_kernel, grid=(part.shape[0] // SENT,), in_specs=[row,...  6.61 us
  transfers between devices with their start and end apart: 12, of which 7 were waited for; matrix products, arithmetic and copies ran while one was open for 7% of the time, Pallas kernels for 13%

profile of v1, /device:TPU:1, one launch (start us, length us, event | category | flops | bytes accessed | tf_op | source)
XLA Modules:
  0.0 186.6 jit_solution(8189543497565957129)
XLA Ops:
  3.1 2.2 %collective-permute-start.1 = (bf16[112,128]{1,0:T(8,128)(2,1)S(1)}, bf16[112,128]{1,0:T(8,128)(2,1)S(1)}, u32[]{:S(2)}, u32[]{:S(2)}) collective-permute-start(bf16[112,128]{1,0:T(8,128)(2,1)S(1)} %bitcast_select_fusion), channel_id=1, source_target_pairs={{0,1},{1,16},{16,17},{17,0},{2,3},{3,18},{18,19},{19,2},{4,5},{5,2... | collective-permute-start | bytes 86024 | tf_op jit(solution)/shard_map/ppermute | solution.py:1067
  5.3 1.5 collective-permute-start.2
  6.8 1.6 collective-permute-start.3
  11.1 1.6 broadcast_in_dim.74
  12.7 7.7 %all-to-all-start = ((bf16[16,4,112,128]{3,2,1,0:T(8,128)(2,1)}), bf16[16,4,112,128]{3,2,1,0:T(8,128)(2,1)S(1)}, u32[]{:S(2)}, u32[]{:S(2)}) async-start(bf16[16,4,112,128]{3,2,1,0:T(8,128)(2,1)} %broadcast_in_dim.74), calls=%async_computation | async-start | bytes 3670016 | tf_op jit(solution)/shard_map/all_to_all | solution.py:1096
  22.4 4.4 %prep.2 = (bf16[4096,256]{1,0:T(8,128)(2,1)}, bf16[4096,256]{1,0:T(8,128)(2,1)}, bf16[4096,256]{1,0:T(8,128)(2,1)}, bf16[256,4096]{1,0:T(8,128)(2,1)}, bf16[256,...) custom-call(bf16[2048,256]{1,0:T(8,128)(2,1)} %bitcast.74, f32[64,128]{1,0:T(8,128)} %get-tuple-element.138.sa, ...), custom_call_target="tpu_custom_call" | custom-call | flops 1000000000 | bytes 8000000 | tf_op jit(solution)/shard_map/prep/pallas_call | solution.py:220
  28.2 4.2 %collective-permute-done.half = bf16[2048,256]{1,0:T(8,128)(2,1)S(1)} collective-permute-done((bf16[2048,256]{1,0:T(8,128)(2,1)}, bf16[2048,256]{1,0:T(8,128)(2,1)S(1)}, u32[]{:S(2)}, u32[]{:S(2)}) %collective-permute-start) | collective-permute-done | bytes 1048608 | tf_op jit(solution)/shard_map/ppermute | solution.py:1087
  33.3 4.4 %prep.3 = (bf16[4096,256]{1,0:T(8,128)(2,1)}, bf16[4096,256]{1,0:T(8,128)(2,1)}, bf16[4096,256]{1,0:T(8,128)(2,1)}, bf16[256,4096]{1,0:T(8,128)(2,1)}, bf16[256,...) custom-call(bf16[2048,256]{1,0:T(8,128)(2,1)} %copy-done.9, ...), custom_call_target="tpu_custom_call", output_to_operand_aliasing={{0}: (5, {}), {1}: (6, {}), {2}: (7, {}), {3}: (8, {}), {4}... | custom-call | flops 1000000000 | bytes 8000000 | tf_op jit(solution)/shard_map/prep/pallas_call | solution.py:220
  37.8 5.2 %all-to-all-done = bf16[16,4,112,128]{3,2,1,0:T(8,128)(2,1)S(1)} async-done(((bf16[16,4,112,128]{3,2,1,0:T(8,128)(2,1)}), bf16[16,4,112,128]{3,2,1,0:T(8,128)(2,1)S(1)}, u32[]{:S(2)}, u32[]{:S(2)}) %all-to-all-start) | async-done | bytes 1835040 | tf_op jit(solution)/shard_map/all_to_all | solution.py:1096
  43.0 5.0 %collective-permute-start.4 = (bf16[64,112,128]{2,1,0:T(8,128)(2,1)S(1)}, bf16[64,112,128]{2,1,0:T(8,128)(2,1)S(1)}, u32[]{:S(2)}, u32[]{:S(2)}) collective-permute-start(bf16[64,112,128]{2,1,0:T(8,128)(2,1)S(1)} %bitcast.59), channel_id=1, source_target_pairs={{0,2},{2,0},{1,3},{3,1},{4,6},{6,4},{5,7},{7,5},{8,10},{10,8},{9,1... | collective-permute-start | bytes 5505032 | tf_op jit(solution)/shard_map/ppermute | solution.py:1075
  47.9 3.4 %collective-permute-done.4.other_h = bf16[64,112,128]{2,1,0:T(8,128)(2,1)S(1)} collective-permute-done((bf16[64,112,128]{2,1,0:T(8,128)(2,1)S(1)}, bf16[64,112,128]{2,1,0:T(8,128)(2,1)S(1)}, u32[]{:S(2)}, u32[]{:S(2)}) %collective-permute-start.4) | collective-permute-done | bytes 1835040 | tf_op jit(solution)/shard_map/ppermute | solution.py:1075
  52.6 15.3 %tokens.1 = (f32[4096,256]{1,0:T(8,128)}, bf16[4608,256]{1,0:T(8,128)(2,1)}, f32[1216,256]{1,0:T(8,128)}, f32[528,128]{1,0:T(8,128)}, bf16[5376,256]{1,0:T(8,128)(2,1)}, /*index=5*/bf16[6,256,128]{2,1,0:T(8,128)(2,1)}) custom-call(s32[8]{0:T(128)} %concatenate.28.place, f32[32,256]{1,0:T(8,128)} %get-tuple-element.79.q0_i, ...), custom_call_target="tpu_custom_call" | custom-call | flops 20000000000 | bytes 30000000 | tf_op jit(solution)/shard_map/tokens/pallas_call | solution.py:476
  68.0 46.7 %image_side.1 = (bf16[4,4096,256]{2,1,0:T(8,128)(2,1)}, f32[2048,256]{1,0:T(8,128)}, s16[544,256]{1,0:T(8,128)(2,1)}, s16[544,256]{1,0:T(8,128)(2,1)}, s16[1088,256]{1,0:T(8,128)(2,1)}, /*index=5*/f32[1560,256]{1,0:T(8,128)}) custom-call(s32[8]{0:T(128)} %concatenate.28.place, bf16[4,4096,256]{2,1,0:T(8,128)(2,1)} %bitcast.72, ...), custom_call_target="tpu_custom_call" | custom-call | flops 49999998976 | bytes 40000000 | tf_op jit(solution)/shard_map/image_side/pallas_call | solution.py:707
  114.8 1.8 copy-done.4
  118.0 5.3 %param_grads.1 = (f32[64,112,128]{2,1,0:T(8,128)S(1)}, f32[64,112,128]{2,1,0:T(8,128)S(1)}, f32[32,256]{1,0:T(8,128)S(1)}) custom-call(s32[8]{0:T(128)S(1)} %copy-done.2, f32[32,256]{1,0:T(8,128)S(1)} %copy-done.1, f32[1216,256]{1,0:T(8,128)S(1)} %copy-done.3, f32[528,128]{1,0:T(8,128)S(1)} %copy-done.7, bf16[6,256,128]{2,1,0:T(8,128)(2,1)S(1)} %copy-done.6, ...), custom_call_target="tpu_custom_call" | custom-call | flops 20000000000 | bytes 10000 | tf_op jit(solution)/shard_map/param_grads/pallas_call | solution.py:926
  125.5 4.6 %collective-permute-done.6.b = f32[64,112,128]{2,1,0:T(8,128)S(1)} collective-permute-done((f32[64,112,128]{2,1,0:T(8,128)S(1)}, f32[64,112,128]{2,1,0:T(8,128)S(1)}, u32[]{:S(2)}, u32[]{:S(2)}) %collective-permute-start.6) | collective-permute-done | bytes 3670048 | tf_op jit(solution)/shard_map/ppermute | solution.py:1075
  132.4 6.0 %all-to-all-start.1 = ((s16[64,112,128]{2,1,0:T(8,128)(2,1)}), s16[64,112,128]{2,1,0:T(8,128)(2,1)S(1)}, u32[]{:S(2)}, u32[]{:S(2)}) async-start(s16[64,112,128]{2,1,0:T(8,128)(2,1)} %copy-done), calls=%async_computation.1 | async-start | bytes 3670016 | tf_op jit(solution)/shard_map/all_to_all | solution.py:1132
  141.8 2.1 %land.3.img = f32[2048,256]{1,0:T(8,128)} custom-call(f32[2048,256]{1,0:T(8,128)} %get-tuple-element.107.img, s16[544,256]{1,0:T(8,128)(2,1)S(1)} %collective-permute-done.5.part), custom_call_target="tpu_custom_call", output_to_operand_aliasing={{}: (0, {})} | custom-call | tf_op jit(solution)/shard_map/land/pallas_call | solution.py:820
  143.9 2.1 %land.4.img = f32[2048,256]{1,0:T(8,128)} custom-call(f32[2048,256]{1,0:T(8,128)} %land.3.img, s16[544,256]{1,0:T(8,128)(2,1)S(1)} %collective-permute-done.7.part), custom_call_target="tpu_custom_call", output_to_operand_aliasing={{}: (0, {})} | custom-call | tf_op jit(solution)/shard_map/land/pallas_call | solution.py:820
  146.0 18.3 %all-to-all-done.1.came = s16[64,112,128]{2,1,0:T(8,128)(2,1)S(1)} async-done(((s16[64,112,128]{2,1,0:T(8,128)(2,1)}), s16[64,112,128]{2,1,0:T(8,128)(2,1)S(1)}, u32[]{:S(2)}, u32[]{:S(2)}) %all-to-all-start.1) | async-done | bytes 1835040 | tf_op jit(solution)/shard_map/all_to_all | solution.py:1132
  165.0 2.0 %settle.1 = (f32[112,128]{1,0:T(8,128)S(1)}, f32[112,128]{1,0:T(8,128)S(1)}, f32[112,128]{1,0:T(8,128)S(1)}, f32[128,1,128]{2,1,0:T(1,128)}) custom-call(s32[4]{0:T(128)S(1)} %pad_add_fusion.where, s16[64,112,128]{2,1,0:T(8,128)(2,1)S(1)} %all-to-all-done.1.came, f32[112,128]{1,0:T(8,128)S(1)} %bitcast.51, f32[112,128]{1,0:T(8,128)S(1)} %bitcast.52, ...), custom_call_target="tpu_custom_call" | custom-call | tf_op jit(solution)/shard_map/settle/pallas_call | solution.py:1000
  167.0 6.4 %all-to-all-start.2 = ((f32[128,1,128]{2,1,0:T(1,128)}), f32[128,1,128]{2,1,0:T(1,128)S(1)}, u32[]{:S(2)}, u32[]{:S(2)}) async-start(f32[128,1,128]{2,1,0:T(1,128)} %get-tuple-element.115), calls=%async_computation.2 | async-start | bytes 131072 | tf_op jit(solution)/shard_map/all_to_all | solution.py:1138
  180.0 2.4 %land.5 = f32[2048,256]{1,0:T(8,128)} custom-call(f32[2048,256]{1,0:T(8,128)} %land.4.img, s16[1088,256]{1,0:T(8,128)(2,1)S(1)} %collective-permute-done.8.part), custom_call_target="tpu_custom_call", output_to_operand_aliasing={{}: (0, {})} | custom-call | tf_op jit(solution)/shard_map/land/pallas_call | solution.py:820
  184.7 1.9 %fusion.16 = (bf16[12336]{0:T(1024)(128)(2,1)}, f32[12336]{0:T(1024)}) fusion(f32[12336]{0:T(1024)S(1)} %copy-done.10, f32[14336]{0:T(1024)S(1)} %bitcast.54, s32[]{:T(128)S(6)} %select_n.129, f32[]{:T(128)} %bitcast.34, f32[]{:T(128)} %bitcast.33, s32[]{:T(128)S(6)} %sub.40), kind=kLoop, calls=%fused_computation.50 | loop fusion | flops 74016 | bytes 172720 | tf_op jit(solution)/shard_map/convert_element_type | solution.py:1156
  (98 shorter events, 25.5 us)
Async XLA Ops:
  3.1 6.6 %collective-permute-start.1 = (bf16[112,128]{1,0:T(8,128)(2,1)S(1)}, bf16[112,128]{1,0:T(8,128)(2,1)S(1)}, u32[]{:S(2)}, u32[]{:S(2)}) collective-permute-start(bf16[112,128]{1,0:T(8,128)(2,1)S(1)} %bitcast_select_fusion), channel_id=1, source_target_pairs={{0,1},{1,16},{16,17},{17,0},{2,3},{3,18},{18,19},{19,2},{4,5},{5,2... | collective-permute-start | bytes 86024 | tf_op jit(solution)/shard_map/ppermute | solution.py:1067
  5.3 4.4 %collective-permute-start.2 = (bf16[112,128]{1,0:T(8,128)(2,1)S(1)}, bf16[112,128]{1,0:T(8,128)(2,1)S(1)}, u32[]{:S(2)}, u32[]{:S(2)}) collective-permute-start(bf16[112,128]{1,0:T(8,128)(2,1)S(1)} %bitcast_select_fusion), channel_id=1, source_target_pairs={{0,17},{1,0},{16,1},{17,16},{2,19},{3,2},{18,3},{19,18},{4,21},{5,... | collective-permute-start | bytes 86024 | tf_op jit(solution)/shard_map/ppermute | solution.py:1067
  6.8 4.2 %collective-permute-start.3 = (bf16[112,128]{1,0:T(8,128)(2,1)S(1)}, bf16[112,128]{1,0:T(8,128)(2,1)S(1)}, u32[]{:S(2)}, u32[]{:S(2)}) collective-permute-start(bf16[112,128]{1,0:T(8,128)(2,1)S(1)} %bitcast_select_fusion), channel_id=1, source_target_pairs={{0,16},{1,17},{16,0},{17,1},{2,18},{3,19},{18,2},{19,3},{4,20},{5,... | collective-permute-start | bytes 86024 | tf_op jit(solution)/shard_map/ppermute | solution.py:1067
  8.4 24.0 %collective-permute-start = (bf16[2048,256]{1,0:T(8,128)(2,1)}, bf16[2048,256]{1,0:T(8,128)(2,1)S(1)}, u32[]{:S(2)}, u32[]{:S(2)}) collective-permute-start(bf16[2048,256]{1,0:T(8,128)(2,1)} %bitcast.73), channel_id=1, source_target_pairs={{0,1},{1,0},{2,3},{3,2},{4,5},{5,4},{6,7},{7,6},{8,9},{9,8},{10,11... | collective-permute-start | bytes 3145736 | tf_op jit(solution)/shard_map/ppermute | solution.py:1087
  12.7 8.1 %copy-start.13 = (bf16[1,4,7,256]{3,1,2,0:T(4,128)(2,1)S(1)}, bf16[1,4,7,256]{3,1,2,0:T(4,128)(2,1)}, u32[]{:S(2)}) copy-start(bf16[1,4,7,256]{3,1,2,0:T(4,128)(2,1)} %param.11) | copy-start | bytes 43012
  12.7 8.1 %copy-start.14 = (bf16[1,4,7,256]{3,1,2,0:T(4,128)(2,1)S(1)}, bf16[1,4,7,256]{3,1,2,0:T(4,128)(2,1)}, u32[]{:S(2)}) copy-start(bf16[1,4,7,256]{3,1,2,0:T(4,128)(2,1)} %param.16) | copy-start | bytes 43012
  12.7 8.2 %copy-start.15 = (s32[1,4]{1,0:T(1,128)S(1)}, s32[1,4]{1,0:T(1,128)}, u32[]{:S(2)}) copy-start(s32[1,4]{1,0:T(1,128)} %param.14) | copy-start | bytes 52
  12.7 30.3 %all-to-all-start = ((bf16[16,4,112,128]{3,2,1,0:T(8,128)(2,1)}), bf16[16,4,112,128]{3,2,1,0:T(8,128)(2,1)S(1)}, u32[]{:S(2)}, u32[]{:S(2)}) async-start(bf16[16,4,112,128]{3,2,1,0:T(8,128)(2,1)} %broadcast_in_dim.74), calls=%async_computation | async-start | bytes 3670016 | tf_op jit(solution)/shard_map/all_to_all | solution.py:1096
  43.0 8.4 %copy-start.8 = (bf16[16,4,112,128]{3,2,1,0:T(8,128)(2,1)}, bf16[16,4,112,128]{3,2,1,0:T(8,128)(2,1)S(1)}, u32[]{:S(2)}) copy-start(bf16[16,4,112,128]{3,2,1,0:T(8,128)(2,1)S(1)} %all-to-all-done) | copy-start | bytes 5505028
  43.0 8.4 %collective-permute-start.4 = (bf16[64,112,128]{2,1,0:T(8,128)(2,1)S(1)}, bf16[64,112,128]{2,1,0:T(8,128)(2,1)S(1)}, u32[]{:S(2)}, u32[]{:S(2)}) collective-permute-start(bf16[64,112,128]{2,1,0:T(8,128)(2,1)S(1)} %bitcast.59), channel_id=1, source_target_pairs={{0,2},{2,0},{1,3},{3,1},{4,6},{6,4},{5,7},{7,5},{8,10},{10,8},{9,1... | collective-permute-start | bytes 5505032 | tf_op jit(solution)/shard_map/ppermute | solution.py:1075
  67.9 46.8 %copy-start.1 = (f32[32,256]{1,0:T(8,128)S(1)}, f32[32,256]{1,0:T(8,128)}, u32[]{:S(2)}) copy-start(f32[32,256]{1,0:T(8,128)} %maximum_maximum_fusion.pe_i) | copy-start | bytes 98308
  67.9 46.8 %copy-start.2 = (s32[8]{0:T(128)S(1)}, s32[8]{0:T(128)}, u32[]{:S(2)}) copy-start(s32[8]{0:T(128)} %concatenate.28.place) | copy-start | bytes 100
  67.9 46.8 %copy-start.3 = (f32[1216,256]{1,0:T(8,128)S(1)}, f32[1216,256]{1,0:T(8,128)}, u32[]{:S(2)}) copy-start(f32[1216,256]{1,0:T(8,128)} %get-tuple-element.85.small_i.refs_0_.a32) | copy-start | bytes 3735556
  67.9 46.8 %copy-start.6 = (bf16[6,256,128]{2,1,0:T(8,128)(2,1)S(1)}, bf16[6,256,128]{2,1,0:T(8,128)(2,1)}, u32[]{:S(2)}) copy-start(bf16[6,256,128]{2,1,0:T(8,128)(2,1)} %get-tuple-element.94.refs_3_.slim) | copy-start | bytes 1179652
  67.9 46.8 %copy-start.7 = (f32[528,128]{1,0:T(8,128)S(1)}, f32[528,128]{1,0:T(8,128)}, u32[]{:S(2)}) copy-start(f32[528,128]{1,0:T(8,128)} %get-tuple-element.92.refs_1_.b32) | copy-start | bytes 811012
  114.6 8.6 %collective-permute-start.5 = (s16[544,256]{1,0:T(8,128)(2,1)}, s16[544,256]{1,0:T(8,128)(2,1)S(1)}, u32[]{:S(2)}, u32[]{:S(2)}) collective-permute-start(s16[544,256]{1,0:T(8,128)(2,1)} %get-tuple-element.100), channel_id=1, source_target_pairs={{0,1},{1,0},{2,3},{3,2},{4,5},{5,4},{6,7},{7,6},{8,9},{9,8},{10,11... | collective-permute-start | bytes 835592 | tf_op jit(solution)/shard_map/ppermute | solution.py:1111
  123.3 6.8 %collective-permute-start.6 = (f32[64,112,128]{2,1,0:T(8,128)S(1)}, f32[64,112,128]{2,1,0:T(8,128)S(1)}, u32[]{:S(2)}, u32[]{:S(2)}) collective-permute-start(f32[64,112,128]{2,1,0:T(8,128)S(1)} %get-tuple-element.102), channel_id=1, source_target_pairs={{0,2},{2,0},{1,3},{3,1},{4,6},{6,4},{5,7},{7,5},{8,10},{10,8},{9,1... | collective-permute-start | bytes 11010056 | tf_op jit(solution)/shard_map/ppermute | solution.py:1075
  124.0 8.4 %collective-permute-start.7 = (s16[544,256]{1,0:T(8,128)(2,1)S(1)}, s16[544,256]{1,0:T(8,128)(2,1)S(1)}, u32[]{:S(2)}, u32[]{:S(2)}) collective-permute-start(s16[544,256]{1,0:T(8,128)(2,1)S(1)} %copy-done.17), channel_id=1, source_target_pairs={{0,1},{1,0},{2,3},{3,2},{4,5},{5,4},{6,7},{7,6},{8,9},{9,8},{10,11... | collective-permute-start | bytes 835592 | tf_op jit(solution)/shard_map/ppermute | solution.py:1113
  132.4 6.8 %copy-start.11 = (f32[12336]{0:T(1024)S(1)}, f32[12336]{0:T(1024)}, u32[]{:S(2)}) copy-start(f32[12336]{0:T(1024)} %param.19) | copy-start | bytes 148036
  132.4 7.4 %copy-start.12 = (f32[12336]{0:T(1024)S(1)}, f32[12336]{0:T(1024)}, u32[]{:S(2)}) copy-start(f32[12336]{0:T(1024)} %param.20) | copy-start | bytes 148036
  132.4 8.0 %copy-start.18 = (s32[14]{0:T(128)S(1)}, s32[14]{0:T(128)}, u32[]{:S(2)}) copy-start(s32[14]{0:T(128)} %constant.156.clone) | copy-start | bytes 172
  132.4 31.9 %all-to-all-start.1 = ((s16[64,112,128]{2,1,0:T(8,128)(2,1)}), s16[64,112,128]{2,1,0:T(8,128)(2,1)S(1)}, u32[]{:S(2)}, u32[]{:S(2)}) async-start(s16[64,112,128]{2,1,0:T(8,128)(2,1)} %copy-done), calls=%async_computation.1 | async-start | bytes 3670016 | tf_op jit(solution)/shard_map/all_to_all | solution.py:1132
  164.3 15.7 %collective-permute-start.8 = (s16[1088,256]{1,0:T(8,128)(2,1)}, s16[1088,256]{1,0:T(8,128)(2,1)S(1)}, u32[]{:S(2)}, u32[]{:S(2)}) collective-permute-start(s16[1088,256]{1,0:T(8,128)(2,1)} %get-tuple-element.117), channel_id=1, source_target_pairs={{0,1},{1,0},{2,3},{3,2},{4,5},{5,4},{6,7},{7,6},{8,9},{9,8},{10,11... | collective-permute-start | bytes 1671176 | tf_op jit(solution)/shard_map/ppermute | solution.py:1136
  167.0 16.3 %all-to-all-start.2 = ((f32[128,1,128]{2,1,0:T(1,128)}), f32[128,1,128]{2,1,0:T(1,128)S(1)}, u32[]{:S(2)}, u32[]{:S(2)}) async-start(f32[128,1,128]{2,1,0:T(1,128)} %get-tuple-element.115), calls=%async_computation.2 | async-start | bytes 131072 | tf_op jit(solution)/shard_map/all_to_all | solution.py:1138
  (7 other events, 18.9 us)

commit v2 on v1

--- a/solution.py
+++ b/solution.py
@@ -56,6 +56,7 @@
 PART0 = (0, 1, 2)
 MIB = 1024 * 1024
 MOST = 58 * MIB
+IMAGE = 55 * MIB
 
 
 def mm(a, b, ca=1, cb=0):
@@ -237,7 +238,7 @@
 NAR, NAR2, RR, VEC, PS, NARROW32 = 0, 32, 128, 224, 272, 528
 SELF, TOW, UOW, UPB, DOWNB, ROWS16 = 0, 1024, 1152, 1280, 3328, 5376
 
-G1, DM2, DF1, DPRE, DVW, DTOK, DNAR, DC2, DOTS, DGAIN, ROWSC = 0, 256, 512, 768, 1024, 1288, 1416, 1512, 1520, 1528, 1560
+DM2, DF1, DPRE, DVW, DTOK, DNAR, DC2, DOTS, DGAIN, DSHIFT, ROWSC = 0, 256, 512, 768, 1032, 1160, 1256, 1264, 1272, 1304, 1312
 
 
 def tok32(ref, row, k):
@@ -277,7 +278,7 @@
 
 def tokens_kernel(
     place, q0_i, pe_i, mine_h, other_h, lh_h, ll_h, k0t_h,
-    s1_h, big_h, a32_h, b32_h, w16_h, slim_h,
+    s1_h, big_h, a32_h, b32_h, w16_h, slim_h, wself_h,
     s1_o, big, a32, b32, w16, slim,
     w_s, notes_s, ut, mine_i, other_i, lh_i, ll_i, k0t_i, sems, sems_out,
 ):
@@ -323,6 +324,14 @@
         w16[SELF + 256 * k : SELF + 256 * k + 256, :] = wide(w_s, at, 256)
     w16[TOW : TOW + 128, :] = wide(w_s, TO, 128)
     w16[UOW : UOW + 128, :] = wide(w_s, UO, 128)
+    for k in range(16):
+        at = UPB + 256 * (k // 2)
+        lanes = slice(128 * (k % 2), 128 * (k % 2) + 128)
+        w16[at : at + 256, lanes] = w_s[pl.ds(UP + k, 256, stride=16), :].astype(BF)
+    for k in range(8):
+        w16[DOWNB + 256 * k : DOWNB + 256 * k + 256, :] = wide(w_s, DOWN + 512 * k, 256)
+    leave(2, w16, w16_h)
+    leave(8, w16.at[SELF : SELF + 1024], wself_h)
 
     def self_w(k):
         return w16[SELF + 256 * k : SELF + 256 * k + 256, :]
@@ -375,13 +384,6 @@
         k0t = k0t_i[:, at]
         part = mm(jnp.concatenate([k0t, k0t], axis=1), jnp.concatenate([eh, el], axis=0))
         ut[...] = part if j == 0 else ut[...] + part
-    for k in range(16):
-        at = UPB + 256 * (k // 2)
-        lanes = slice(128 * (k % 2), 128 * (k % 2) + 128)
-        w16[at : at + 256, lanes] = w_s[pl.ds(UP + k, 256, stride=16), :].astype(BF)
-    for k in range(8):
-        w16[DOWNB + 256 * k : DOWNB + 256 * k + 256, :] = wide(w_s, DOWN + 512 * k, 256)
-    leave(2, w16, w16_h)
     inverse = 1.0 / total
     a32[STAT : STAT + 1, :] = top
     a32[STAT + 1 : STAT + 2, :] = inverse
@@ -478,8 +480,8 @@
         in_specs=[pl.BlockSpec(memory_space=pltpu.SMEM)]
         + in_vmem(2)
         + [pl.BlockSpec(memory_space=pl.ANY)] * 5,
-        out_specs=[pl.BlockSpec(memory_space=pl.ANY)] * len(out),
-        out_shape=specs(out),
+        out_specs=[pl.BlockSpec(memory_space=pl.ANY)] * (len(out) + 1),
+        out_shape=specs(out + [((1024, 256), BF)]),
         scratch_shapes=[pltpu.VMEM(shape, t) for shape, t in out]
         + [
             pltpu.VMEM((PADDED, 128), F32),
@@ -491,7 +493,7 @@
             pltpu.VMEM((IMG, D), BF),
             pltpu.VMEM((D, IMG), BF),
             pltpu.SemaphoreType.DMA((11,)),
-            pltpu.SemaphoreType.DMA((len(out) + 2,)),
+            pltpu.SemaphoreType.DMA((len(out) + 3,)),
         ],
         compiler_params=pltpu.CompilerParams(vmem_limit_bytes=MOST),
         cost_estimate=pl.CostEstimate(flops=2 * 10**10, bytes_accessed=3 * 10**7, transcendentals=0),
@@ -529,7 +531,7 @@
 def image_steps(
     place, cot_i, k0_i, lh_i, ll_i, lht_i, llt_i, s1_i, big_i, small_i, cq_i, a32, b32, w16, slim, later,
     keys_o, img_o, part0_o, part1_o, part2_o, c32,
-    s_s, p_s, left_s, b_s, n_s, r_s, x_s, kc_s, acc, g2_o, dut, both,
+    s_s, p_s, left_s, b_s, n_s, r_s, x_s, kc_s, acc, g1_o, g2_o, dut, both,
 ):
     j = pl.program_id(0)
 
@@ -538,13 +540,14 @@
         for copy in later:
             copy.start()
         c32[...] = jnp.zeros((ROWSC, 256), F32)
+        g1_o[...] = jnp.zeros(g1_o.shape, F32)
         g2_o[...] = jnp.zeros(g2_o.shape, F32)
 
     @pl.when(j < STEPS_I)
     def _():
         image_part(
             cot_i, k0_i, lh_i, ll_i, lht_i, llt_i, big_i, small_i, keys_o,
-            acc.at[pl.ds(pl.multiple_of(j * TI, TI), TI)], c32, g2_o,
+            acc.at[pl.ds(pl.multiple_of(j * TI, TI), TI)], c32, g1_o, g2_o,
             s_s, p_s, left_s, b_s, n_s, r_s, x_s, kc_s,
         )
 
@@ -552,7 +555,7 @@
     def _():
         for copy in later:
             copy.wait()
-        chain_part(cq_i, a32, b32, w16, slim, c32, g2_o, dut, both)
+        chain_part(cq_i, a32, b32, w16, slim, c32, g1_o, g2_o, dut, both)
 
     def step(at, keep):
         image_step(
@@ -573,7 +576,7 @@
 
 
 def image_part(
-    cot_i, k0_i, lh_i, ll_i, lht_i, llt_i, big_i, small_i, keys_o, acc_o, c32, g2_o,
+    cot_i, k0_i, lh_i, ll_i, lht_i, llt_i, big_i, small_i, keys_o, acc_o, c32, g1_o, g2_o,
     s_s, p_s, left_s, b_s, n_s, r_s, x_s, kc_s,
 ):
     lh = lh_i[...]
@@ -672,7 +675,7 @@
         pick = [l1[32 * i + 8 * b : 32 * i + 8 * b + 8] for i in range(8)]
         hi, lo = split(jnp.concatenate(pick, axis=0))
         y = mm(jnp.concatenate([hi, lo], axis=0), cot_i[b])
-        c32[G1 + 64 * b : G1 + 64 * b + 64, :] += y[:64] + y[64:]
+        g1_o[b] += y[:64] + y[64:]
         g2_o[b] += mm(hi, n_s[b])
 
 
@@ -724,6 +727,7 @@
                 pltpu.VMEM((TI, 256), F32),
                 pltpu.VMEM((IMG, 256), F32),
                 pltpu.VMEM((4, 64, 256), F32),
+                pltpu.VMEM((4, 64, 256), F32),
                 pltpu.VMEM((512, 256), BF),
                 pltpu.VMEM((1536, 256), BF),
             ]
@@ -731,7 +735,7 @@
             + [pltpu.SemaphoreType.DMA((len(whole),))],
         ),
         out_shape=specs(out),
-        compiler_params=pltpu.CompilerParams(vmem_limit_bytes=MOST),
+        compiler_params=pltpu.CompilerParams(vmem_limit_bytes=IMAGE),
         cost_estimate=pl.CostEstimate(flops=5 * 10**10, bytes_accessed=4 * 10**7, transcendentals=0),
         name="image_side",
     )(place, cot, k0, lh, ll, lht, llt, s1, big, a32, cq, *whole)
@@ -762,14 +766,16 @@
         ref[TC + 16 * part : TC + 16 * part + 16, :] = k[:, D * part : D * part + D]
 
 
-def chain_part(cq_i, a32, b32, w16, slim, c32, g2_i, dut, both):
+def chain_part(cq_i, a32, b32, w16, slim, c32, g1_i, g2_i, dut, both):
     m128 = head_mask(INNER)
     scale1 = 1.0 / math.sqrt(INNER // HEADS)
     vec = b32.at[VEC : VEC + VROWS]
     per_box = []
     for b in range(4):
         gain = a32[SMALL + 8 + b : SMALL + 9 + b, :]
-        x = c32[G1 + 64 * b : G1 + 64 * b + 64, :] * gain - g2_i[b]
+        raw = g1_i[b]
+        c32[DSHIFT + b : DSHIFT + b + 1, :] = raw[57:58]
+        x = raw * gain - g2_i[b]
         per_box.append(x - jnp.mean(x, axis=1, keepdims=True))
     bo_sum = sum(x[56:57] for x in per_box)
     zero = jnp.zeros((8, 256), F32)
@@ -840,12 +846,10 @@
 
 
 def grads_kernel(
-    place, pe_i, a32, b32, slim, c32, w16_h,
+    place, pe_i, a32, b32, slim, c32, self_i,
     mine_o, other_o, dq_o,
-    gm_o, self_i, sem,
+    gm_o,
 ):
-    weights = pltpu.make_async_copy(w16_h.at[SELF : SELF + 1024], self_i, sem)
-    weights.start()
     vec = b32.at[VEC : VEC + VROWS]
     m128 = head_mask(INNER)
     scale1 = 1.0 / math.sqrt(INNER // HEADS)
@@ -871,7 +875,7 @@
     vput("g2", col_sum(dq2 * n2))
     vput("h2", col_sum(dq2))
     vput("u_bo", c32[DVW + 256 : DVW + 257, :])
-    vput("h4", sum(c32[G1 + 64 * b + 57 : G1 + 64 * b + 58, :] * a32[WT + b : WT + b + 1, :] for b in range(4)))
+    vput("h4", sum(c32[DSHIFT + b : DSHIFT + b + 1, :] * a32[WT + b : WT + b + 1, :] for b in range(4)))
     vput("g4", sum(col_sum(c32[DGAIN + 8 * b : DGAIN + 8 * b + 8, :]) * a32[WT + b : WT + b + 1, :] for b in range(4)))
     pack256(gm_o, UO, mm3(expand(v2, m128), c32[DVW : DVW + 256, :], 0, 0))
     k2x = expand(k2, m128)
@@ -896,7 +900,6 @@
     dx1 = ln_back(dq1, n1, b32[RR : RR + 32, 0:1], vget(vec, "g1"))
     m256 = head_mask(D)
     scale = 1.0 / math.sqrt(D // HEADS)
-    weights.wait()
     vput("s_bo", col_sum(dx1))
     pack256(gm_o, SO, outer(o, dx1))
     do = expand(mm_w(dx1, self_i[768:1024, :], 1), m256)
@@ -926,14 +929,9 @@
     return pl.pallas_call(
         grads_kernel,
         in_specs=[pl.BlockSpec(memory_space=pltpu.SMEM)]
-        + in_vmem(len(args) - 2)
-        + [pl.BlockSpec(memory_space=pl.ANY)],
+        + in_vmem(len(args) - 1),
         out_specs=in_vmem(3),
-        scratch_shapes=[
-            pltpu.VMEM((PADDED, 128), F32),
-            pltpu.VMEM((1024, 256), BF),
-            pltpu.SemaphoreType.DMA,
-        ],
+        scratch_shapes=[pltpu.VMEM((PADDED, 128), F32)],
         out_shape=specs([((PEERS, CHUNK, 128), F32), ((PEERS, CHUNK, 128), F32), ((32, 256), F32)]),
         compiler_params=pltpu.CompilerParams(vmem_limit_bytes=12 * MIB),
         cost_estimate=pl.CostEstimate(flops=2 * 10**10, bytes_accessed=10**4, transcendentals=0),
@@ -1048,12 +1046,12 @@
     cq = by_token(cot_q.astype(F32))
     place, ready, pe, q0, cq, mine = lax.optimization_barrier((place, ready, pe, q0, cq, mine))
     k0, lh, ll, lht, llt, k0t = ready
-    s1, big, a32, b32, w16, slim = tokens(place, q0, pe, mine, swap(mine), lh, ll, k0t)
+    s1, big, a32, b32, w16, slim, wself = tokens(place, q0, pe, mine, swap(mine), lh, ll, k0t)
     keys, img, one, two, three, c32 = image_side(
         place, cot_k, k0, lh, ll, lht, llt, s1, big, cq, a32, b32, w16, slim
     )
     parts = one, two, three
-    gmine, gother, dq = param_grads(place, pe, a32, b32, slim, c32, w16)
+    gmine, gother, dq = param_grads(place, pe, a32, b32, slim, c32, wself)
     queries_out = a32[TOK2 + 96 : TOK2 + 128]
     return by_box(queries_out).astype(BF), keys, by_box(dq), img, parts, gmine, gother
 

time: 188 us -> 187 us (level)
  waiting for transfers between devices: 37.9 us -> 41 us
  starting transfers between devices: 33.7 us -> 31.6 us
  local copies, waits for them, and re-layouts: 15 us -> 13.1 us
  transfers between devices with their start and end apart: 12 -> 12, of which waited for: 7 -> 8; matrix products, arithmetic and copies ran while one was open for 7% -> 7% of each run, Pallas kernels for 13% -> 13%
where the time goes in v2:
time: 187 us; the launch traced here: 186 us
  Pallas kernels  86.2 us (46%)
  waiting for transfers between devices  41 us (22%)
  starting transfers between devices  31.6 us (17%)
  local copies, waits for them, and re-layouts  13.1 us (7%)
  other arithmetic  9.04 us (5%)
  between operations  5.1 us (3%)
    pallas_call x1, Pallas kernels, image_side(): pl.pallas_call(image_kernel, grid_spec=pltpu.PrefetchScalarGridSpec(num_s...  46.6 us
    all_to_all x1, waiting for transfers between devices, local(): came = lax.all_to_all(sent, HALFWAY, 0, 0, tiled=True)  18.4 us
    pallas_call x1, Pallas kernels, tokens(): pl.pallas_call(tokens_kernel, in_specs=[pl.BlockSpec(memory_space=pltpu.S...  15.8 us
    ppermute x2, waiting for transfers between devices, swap(): return lax.ppermute(x, 'cuts_3', SWAP)  9.44 us
    pallas_call x2, Pallas kernels, prep(): pl.pallas_call(prep_kernel, grid=(HALF,), in_specs=[pl.BlockSpec((TC, D),...  8.88 us
    all_to_all x1, starting transfers between devices, local(): lax.all_to_all(jnp.broadcast_to(column[None], (PEERS // 4, 4, CHUNK, 128)...  7.73 us
    pallas_call x3, Pallas kernels, land(): pl.pallas_call(land_kernel, grid=(part.shape[0] // SENT,), in_specs=[row,...  6.61 us
    all_to_all x1, starting transfers between devices, local(): squares = lax.all_to_all(squares, CUTS_BOX, 0, 0, tiled=True)  6.3 us
  transfers between devices with their start and end apart: 12, of which 8 were waited for; matrix products, arithmetic and copies ran while one was open for 7% of the time, Pallas kernels for 13%

profile of v2, /device:TPU:1, one launch (start us, length us, event | category | flops | bytes accessed | tf_op | source)
XLA Modules:
  0.0 186.1 jit_solution(1321449375743077850)
XLA Ops:
  3.1 2.2 %collective-permute-start.1 = (bf16[112,128]{1,0:T(8,128)(2,1)S(1)}, bf16[112,128]{1,0:T(8,128)(2,1)S(1)}, u32[]{:S(2)}, u32[]{:S(2)}) collective-permute-start(bf16[112,128]{1,0:T(8,128)(2,1)S(1)} %bitcast_select_fusion), channel_id=1, source_target_pairs={{0,1},{1,16},{16,17},{17,0},{2,3},{3,18},{18,19},{19,2},{4,5},{5,2... | collective-permute-start | bytes 86024 | tf_op jit(solution)/shard_map/ppermute | solution.py:1065
  5.3 1.5 collective-permute-start.2
  6.8 1.6 collective-permute-start.3
  11.1 1.6 broadcast_in_dim.74
  12.7 7.7 %all-to-all-start = ((bf16[16,4,112,128]{3,2,1,0:T(8,128)(2,1)}), bf16[16,4,112,128]{3,2,1,0:T(8,128)(2,1)S(1)}, u32[]{:S(2)}, u32[]{:S(2)}) async-start(bf16[16,4,112,128]{3,2,1,0:T(8,128)(2,1)} %broadcast_in_dim.74), calls=%async_computation | async-start | bytes 3670016 | tf_op jit(solution)/shard_map/all_to_all | solution.py:1094
  22.4 4.4 %prep.2 = (bf16[4096,256]{1,0:T(8,128)(2,1)}, bf16[4096,256]{1,0:T(8,128)(2,1)}, bf16[4096,256]{1,0:T(8,128)(2,1)}, bf16[256,4096]{1,0:T(8,128)(2,1)}, bf16[256,...) custom-call(bf16[2048,256]{1,0:T(8,128)(2,1)} %bitcast.74, f32[64,128]{1,0:T(8,128)} %get-tuple-element.140.sa, ...), custom_call_target="tpu_custom_call" | custom-call | flops 1000000000 | bytes 8000000 | tf_op jit(solution)/shard_map/prep/pallas_call | solution.py:221
  28.2 4.2 %collective-permute-done.half = bf16[2048,256]{1,0:T(8,128)(2,1)S(1)} collective-permute-done((bf16[2048,256]{1,0:T(8,128)(2,1)}, bf16[2048,256]{1,0:T(8,128)(2,1)S(1)}, u32[]{:S(2)}, u32[]{:S(2)}) %collective-permute-start) | collective-permute-done | bytes 1048608 | tf_op jit(solution)/shard_map/ppermute | solution.py:1085
  33.3 4.4 %prep.3 = (bf16[4096,256]{1,0:T(8,128)(2,1)}, bf16[4096,256]{1,0:T(8,128)(2,1)}, bf16[4096,256]{1,0:T(8,128)(2,1)}, bf16[256,4096]{1,0:T(8,128)(2,1)}, bf16[256,...) custom-call(bf16[2048,256]{1,0:T(8,128)(2,1)} %copy-done.9, ...), custom_call_target="tpu_custom_call", output_to_operand_aliasing={{0}: (5, {}), {1}: (6, {}), {2}: (7, {}), {3}: (8, {}), {4}... | custom-call | flops 1000000000 | bytes 8000000 | tf_op jit(solution)/shard_map/prep/pallas_call | solution.py:221
  37.8 5.2 %all-to-all-done = bf16[16,4,112,128]{3,2,1,0:T(8,128)(2,1)S(1)} async-done(((bf16[16,4,112,128]{3,2,1,0:T(8,128)(2,1)}), bf16[16,4,112,128]{3,2,1,0:T(8,128)(2,1)S(1)}, u32[]{:S(2)}, u32[]{:S(2)}) %all-to-all-start) | async-done | bytes 1835040 | tf_op jit(solution)/shard_map/all_to_all | solution.py:1094
  43.0 5.0 %collective-permute-start.4 = (bf16[64,112,128]{2,1,0:T(8,128)(2,1)S(1)}, bf16[64,112,128]{2,1,0:T(8,128)(2,1)S(1)}, u32[]{:S(2)}, u32[]{:S(2)}) collective-permute-start(bf16[64,112,128]{2,1,0:T(8,128)(2,1)S(1)} %bitcast.59), channel_id=1, source_target_pairs={{0,2},{2,0},{1,3},{3,1},{4,6},{6,4},{5,7},{7,5},{8,10},{10,8},{9,1... | collective-permute-start | bytes 5505032 | tf_op jit(solution)/shard_map/ppermute | solution.py:1073
  47.9 3.4 %collective-permute-done.4.other_h = bf16[64,112,128]{2,1,0:T(8,128)(2,1)S(1)} collective-permute-done((bf16[64,112,128]{2,1,0:T(8,128)(2,1)S(1)}, bf16[64,112,128]{2,1,0:T(8,128)(2,1)S(1)}, u32[]{:S(2)}, u32[]{:S(2)}) %collective-permute-start.4) | collective-permute-done | bytes 1835040 | tf_op jit(solution)/shard_map/ppermute | solution.py:1073
  52.6 15.8 %tokens.1 = (f32[4096,256]{1,0:T(8,128)}, bf16[4608,256]{1,0:T(8,128)(2,1)}, f32[1216,256]{1,0:T(8,128)}, f32[528,128]{1,0:T(8,128)}, bf16[5376,256]{1,0:T(8,128...) custom-call(s32[8]{0:T(128)} %concatenate.28.place, f32[32,256]{1,0:T(8,128)} %get-tuple-element.80.q0_i, ...), custom_call_target="tpu_custom_call" | custom-call | flops 20000000000 | bytes 30000000 | tf_op jit(solution)/shard_map/tokens/pallas_call | solution.py:478
  68.5 46.6 %image_side.1 = (bf16[4,4096,256]{2,1,0:T(8,128)(2,1)}, f32[2048,256]{1,0:T(8,128)}, s16[544,256]{1,0:T(8,128)(2,1)}, s16[544,256]{1,0:T(8,128)(2,1)}, s16[1088,256]{1,0:T(8,128)(2,1)}, /*index=5*/f32[1312,256]{1,0:T(8,128)}) custom-call(s32[8]{0:T(128)} %concatenate.28.place, bf16[4,4096,256]{2,1,0:T(8,128)(2,1)} %bitcast.72, ...), custom_call_target="tpu_custom_call" | custom-call | flops 49999998976 | bytes 40000000 | tf_op jit(solution)/shard_map/image_side/pallas_call | solution.py:710
  116.6 5.2 %param_grads.1 = (f32[64,112,128]{2,1,0:T(8,128)S(1)}, f32[64,112,128]{2,1,0:T(8,128)S(1)}, f32[32,256]{1,0:T(8,128)S(1)}) custom-call(s32[8]{0:T(128)S(1)} %copy-done.2, f32[32,256]{1,0:T(8,128)S(1)} %copy-done.1, f32[1216,256]{1,0:T(8,128)S(1)} %copy-done.3, f32[528,128]{1,0:T(8,128)S(1)} %copy-done.7, bf16[6,256,128]{2,1,0:T(8,128)(2,1)S(1)} %copy-done.6, ...), custom_call_target="tpu_custom_call" | custom-call | flops 20000000000 | bytes 10000 | tf_op jit(solution)/shard_map/param_grads/pallas_call | solution.py:929
  121.8 1.5 collective-permute-done.5.part
  124.5 6.0 %collective-permute-done.6.b = f32[64,112,128]{2,1,0:T(8,128)S(1)} collective-permute-done((f32[64,112,128]{2,1,0:T(8,128)S(1)}, f32[64,112,128]{2,1,0:T(8,128)S(1)}, u32[]{:S(2)}, u32[]{:S(2)}) %collective-permute-start.6) | collective-permute-done | bytes 3670048 | tf_op jit(solution)/shard_map/ppermute | solution.py:1073
  132.9 5.0 %all-to-all-start.1 = ((s16[64,112,128]{2,1,0:T(8,128)(2,1)}), s16[64,112,128]{2,1,0:T(8,128)(2,1)S(1)}, u32[]{:S(2)}, u32[]{:S(2)}) async-start(s16[64,112,128]{2,1,0:T(8,128)(2,1)} %copy-done), calls=%async_computation.1 | async-start | bytes 3670016 | tf_op jit(solution)/shard_map/all_to_all | solution.py:1130
  141.3 2.1 %land.3.img = f32[2048,256]{1,0:T(8,128)} custom-call(f32[2048,256]{1,0:T(8,128)} %get-tuple-element.109.img, s16[544,256]{1,0:T(8,128)(2,1)S(1)} %collective-permute-done.5.part), custom_call_target="tpu_custom_call", output_to_operand_aliasing={{}: (0, {})} | custom-call | tf_op jit(solution)/shard_map/land/pallas_call | solution.py:826
  143.4 2.1 %land.4.img = f32[2048,256]{1,0:T(8,128)} custom-call(f32[2048,256]{1,0:T(8,128)} %land.3.img, s16[544,256]{1,0:T(8,128)(2,1)S(1)} %collective-permute-done.7.part), custom_call_target="tpu_custom_call", output_to_operand_aliasing={{}: (0, {})} | custom-call | tf_op jit(solution)/shard_map/land/pallas_call | solution.py:826
  145.5 18.4 %all-to-all-done.1.came = s16[64,112,128]{2,1,0:T(8,128)(2,1)S(1)} async-done(((s16[64,112,128]{2,1,0:T(8,128)(2,1)}), s16[64,112,128]{2,1,0:T(8,128)(2,1)S(1)}, u32[]{:S(2)}, u32[]{:S(2)}) %all-to-all-start.1) | async-done | bytes 1835040 | tf_op jit(solution)/shard_map/all_to_all | solution.py:1130
  164.5 2.0 %settle.1 = (f32[112,128]{1,0:T(8,128)S(1)}, f32[112,128]{1,0:T(8,128)S(1)}, f32[112,128]{1,0:T(8,128)S(1)}, f32[128,1,128]{2,1,0:T(1,128)}) custom-call(s32[4]{0:T(128)S(1)} %pad_add_fusion.where, s16[64,112,128]{2,1,0:T(8,128)(2,1)S(1)} %all-to-all-done.1.came, f32[112,128]{1,0:T(8,128)S(1)} %bitcast.51, f32[112,128]{1,0:T(8,128)S(1)} %bitcast.52, ...), custom_call_target="tpu_custom_call" | custom-call | tf_op jit(solution)/shard_map/settle/pallas_call | solution.py:998
  166.5 6.3 %all-to-all-start.2 = ((f32[128,1,128]{2,1,0:T(1,128)}), f32[128,1,128]{2,1,0:T(1,128)S(1)}, u32[]{:S(2)}, u32[]{:S(2)}) async-start(f32[128,1,128]{2,1,0:T(1,128)} %get-tuple-element.117), calls=%async_computation.2 | async-start | bytes 131072 | tf_op jit(solution)/shard_map/all_to_all | solution.py:1136
  179.4 2.4 %land.5 = f32[2048,256]{1,0:T(8,128)} custom-call(f32[2048,256]{1,0:T(8,128)} %land.4.img, s16[1088,256]{1,0:T(8,128)(2,1)S(1)} %collective-permute-done.8.part), custom_call_target="tpu_custom_call", output_to_operand_aliasing={{}: (0, {})} | custom-call | tf_op jit(solution)/shard_map/land/pallas_call | solution.py:826
  184.1 1.9 %fusion.16 = (bf16[12336]{0:T(1024)(128)(2,1)}, f32[12336]{0:T(1024)}) fusion(f32[12336]{0:T(1024)S(1)} %copy-done.10, f32[14336]{0:T(1024)S(1)} %bitcast.54, s32[]{:T(128)S(6)} %select_n.129, f32[]{:T(128)} %bitcast.34, f32[]{:T(128)} %bitcast.33, s32[]{:T(128)S(6)} %sub.40), kind=kLoop, calls=%fused_computation.50 | loop fusion | flops 74016 | bytes 172720 | tf_op jit(solution)/shard_map/convert_element_type | solution.py:1154
  (98 shorter events, 24.3 us)
Async XLA Ops:
  3.1 6.6 %collective-permute-start.1 = (bf16[112,128]{1,0:T(8,128)(2,1)S(1)}, bf16[112,128]{1,0:T(8,128)(2,1)S(1)}, u32[]{:S(2)}, u32[]{:S(2)}) collective-permute-start(bf16[112,128]{1,0:T(8,128)(2,1)S(1)} %bitcast_select_fusion), channel_id=1, source_target_pairs={{0,1},{1,16},{16,17},{17,0},{2,3},{3,18},{18,19},{19,2},{4,5},{5,2... | collective-permute-start | bytes 86024 | tf_op jit(solution)/shard_map/ppermute | solution.py:1065
  5.3 4.4 %collective-permute-start.2 = (bf16[112,128]{1,0:T(8,128)(2,1)S(1)}, bf16[112,128]{1,0:T(8,128)(2,1)S(1)}, u32[]{:S(2)}, u32[]{:S(2)}) collective-permute-start(bf16[112,128]{1,0:T(8,128)(2,1)S(1)} %bitcast_select_fusion), channel_id=1, source_target_pairs={{0,17},{1,0},{16,1},{17,16},{2,19},{3,2},{18,3},{19,18},{4,21},{5,... | collective-permute-start | bytes 86024 | tf_op jit(solution)/shard_map/ppermute | solution.py:1065
  6.8 4.2 %collective-permute-start.3 = (bf16[112,128]{1,0:T(8,128)(2,1)S(1)}, bf16[112,128]{1,0:T(8,128)(2,1)S(1)}, u32[]{:S(2)}, u32[]{:S(2)}) collective-permute-start(bf16[112,128]{1,0:T(8,128)(2,1)S(1)} %bitcast_select_fusion), channel_id=1, source_target_pairs={{0,16},{1,17},{16,0},{17,1},{2,18},{3,19},{18,2},{19,3},{4,20},{5,... | collective-permute-start | bytes 86024 | tf_op jit(solution)/shard_map/ppermute | solution.py:1065
  8.4 24.0 %collective-permute-start = (bf16[2048,256]{1,0:T(8,128)(2,1)}, bf16[2048,256]{1,0:T(8,128)(2,1)S(1)}, u32[]{:S(2)}, u32[]{:S(2)}) collective-permute-start(bf16[2048,256]{1,0:T(8,128)(2,1)} %bitcast.73), channel_id=1, source_target_pairs={{0,1},{1,0},{2,3},{3,2},{4,5},{5,4},{6,7},{7,6},{8,9},{9,8},{10,11... | collective-permute-start | bytes 3145736 | tf_op jit(solution)/shard_map/ppermute | solution.py:1085
  12.7 8.1 %copy-start.13 = (bf16[1,4,7,256]{3,1,2,0:T(4,128)(2,1)S(1)}, bf16[1,4,7,256]{3,1,2,0:T(4,128)(2,1)}, u32[]{:S(2)}) copy-start(bf16[1,4,7,256]{3,1,2,0:T(4,128)(2,1)} %param.11) | copy-start | bytes 43012
  12.7 8.1 %copy-start.14 = (bf16[1,4,7,256]{3,1,2,0:T(4,128)(2,1)S(1)}, bf16[1,4,7,256]{3,1,2,0:T(4,128)(2,1)}, u32[]{:S(2)}) copy-start(bf16[1,4,7,256]{3,1,2,0:T(4,128)(2,1)} %param.16) | copy-start | bytes 43012
  12.7 8.2 %copy-start.15 = (s32[1,4]{1,0:T(1,128)S(1)}, s32[1,4]{1,0:T(1,128)}, u32[]{:S(2)}) copy-start(s32[1,4]{1,0:T(1,128)} %param.14) | copy-start | bytes 52
  12.7 30.3 %all-to-all-start = ((bf16[16,4,112,128]{3,2,1,0:T(8,128)(2,1)}), bf16[16,4,112,128]{3,2,1,0:T(8,128)(2,1)S(1)}, u32[]{:S(2)}, u32[]{:S(2)}) async-start(bf16[16,4,112,128]{3,2,1,0:T(8,128)(2,1)} %broadcast_in_dim.74), calls=%async_computation | async-start | bytes 3670016 | tf_op jit(solution)/shard_map/all_to_all | solution.py:1094
  43.0 8.4 %copy-start.8 = (bf16[16,4,112,128]{3,2,1,0:T(8,128)(2,1)}, bf16[16,4,112,128]{3,2,1,0:T(8,128)(2,1)S(1)}, u32[]{:S(2)}) copy-start(bf16[16,4,112,128]{3,2,1,0:T(8,128)(2,1)S(1)} %all-to-all-done) | copy-start | bytes 5505028
  43.0 8.4 %collective-permute-start.4 = (bf16[64,112,128]{2,1,0:T(8,128)(2,1)S(1)}, bf16[64,112,128]{2,1,0:T(8,128)(2,1)S(1)}, u32[]{:S(2)}, u32[]{:S(2)}) collective-permute-start(bf16[64,112,128]{2,1,0:T(8,128)(2,1)S(1)} %bitcast.59), channel_id=1, source_target_pairs={{0,2},{2,0},{1,3},{3,1},{4,6},{6,4},{5,7},{7,5},{8,10},{10,8},{9,1... | collective-permute-start | bytes 5505032 | tf_op jit(solution)/shard_map/ppermute | solution.py:1073
  68.4 46.8 %copy-start.1 = (f32[32,256]{1,0:T(8,128)S(1)}, f32[32,256]{1,0:T(8,128)}, u32[]{:S(2)}) copy-start(f32[32,256]{1,0:T(8,128)} %maximum_maximum_fusion.pe_i) | copy-start | bytes 98308
  68.5 46.8 %copy-start.2 = (s32[8]{0:T(128)S(1)}, s32[8]{0:T(128)}, u32[]{:S(2)}) copy-start(s32[8]{0:T(128)} %concatenate.28.place) | copy-start | bytes 100
  68.5 46.8 %copy-start.3 = (f32[1216,256]{1,0:T(8,128)S(1)}, f32[1216,256]{1,0:T(8,128)}, u32[]{:S(2)}) copy-start(f32[1216,256]{1,0:T(8,128)} %get-tuple-element.86.small_i.refs_0_.a32) | copy-start | bytes 3735556
  68.5 46.8 %copy-start.5 = (bf16[1024,256]{1,0:T(8,128)(2,1)S(1)}, bf16[1024,256]{1,0:T(8,128)(2,1)}, u32[]{:S(2)}) copy-start(bf16[1024,256]{1,0:T(8,128)(2,1)} %get-tuple-element.98.self_i) | copy-start | bytes 1572868
  68.5 46.8 %copy-start.6 = (bf16[6,256,128]{2,1,0:T(8,128)(2,1)S(1)}, bf16[6,256,128]{2,1,0:T(8,128)(2,1)}, u32[]{:S(2)}) copy-start(bf16[6,256,128]{2,1,0:T(8,128)(2,1)} %get-tuple-element.95.refs_3_.slim) | copy-start | bytes 1179652
  68.5 46.8 %copy-start.7 = (f32[528,128]{1,0:T(8,128)S(1)}, f32[528,128]{1,0:T(8,128)}, u32[]{:S(2)}) copy-start(f32[528,128]{1,0:T(8,128)} %get-tuple-element.93.refs_1_.b32) | copy-start | bytes 811012
  115.1 8.2 %collective-permute-start.5 = (s16[544,256]{1,0:T(8,128)(2,1)}, s16[544,256]{1,0:T(8,128)(2,1)S(1)}, u32[]{:S(2)}, u32[]{:S(2)}) collective-permute-start(s16[544,256]{1,0:T(8,128)(2,1)} %get-tuple-element.102), channel_id=1, source_target_pairs={{0,1},{1,0},{2,3},{3,2},{4,5},{5,4},{6,7},{7,6},{8,9},{9,8},{10,11... | collective-permute-start | bytes 835592 | tf_op jit(solution)/shard_map/ppermute | solution.py:1109
  116.6 7.9 %copy-start.17 = (s16[544,256]{1,0:T(8,128)(2,1)S(1)}, s16[544,256]{1,0:T(8,128)(2,1)}, u32[]{:S(2)}) copy-start(s16[544,256]{1,0:T(8,128)(2,1)} %get-tuple-element.105) | copy-start | bytes 835588
  123.3 7.2 %collective-permute-start.6 = (f32[64,112,128]{2,1,0:T(8,128)S(1)}, f32[64,112,128]{2,1,0:T(8,128)S(1)}, u32[]{:S(2)}, u32[]{:S(2)}) collective-permute-start(f32[64,112,128]{2,1,0:T(8,128)S(1)} %get-tuple-element.104), channel_id=1, source_target_pairs={{0,2},{2,0},{1,3},{3,1},{4,6},{6,4},{5,7},{7,5},{8,10},{10,8},{9,1... | collective-permute-start | bytes 11010056 | tf_op jit(solution)/shard_map/ppermute | solution.py:1073
  124.5 8.4 %collective-permute-start.7 = (s16[544,256]{1,0:T(8,128)(2,1)S(1)}, s16[544,256]{1,0:T(8,128)(2,1)S(1)}, u32[]{:S(2)}, u32[]{:S(2)}) collective-permute-start(s16[544,256]{1,0:T(8,128)(2,1)S(1)} %copy-done.17), channel_id=1, source_target_pairs={{0,1},{1,0},{2,3},{3,2},{4,5},{5,4},{6,7},{7,6},{8,9},{9,8},{10,11... | collective-permute-start | bytes 835592 | tf_op jit(solution)/shard_map/ppermute | solution.py:1111
  132.9 7.0 %copy-start.18 = (s32[14]{0:T(128)S(1)}, s32[14]{0:T(128)}, u32[]{:S(2)}) copy-start(s32[14]{0:T(128)} %constant.156.clone) | copy-start | bytes 172
  132.9 31.0 %all-to-all-start.1 = ((s16[64,112,128]{2,1,0:T(8,128)(2,1)}), s16[64,112,128]{2,1,0:T(8,128)(2,1)S(1)}, u32[]{:S(2)}, u32[]{:S(2)}) async-start(s16[64,112,128]{2,1,0:T(8,128)(2,1)} %copy-done), calls=%async_computation.1 | async-start | bytes 3670016 | tf_op jit(solution)/shard_map/all_to_all | solution.py:1130
  163.9 15.5 %collective-permute-start.8 = (s16[1088,256]{1,0:T(8,128)(2,1)}, s16[1088,256]{1,0:T(8,128)(2,1)S(1)}, u32[]{:S(2)}, u32[]{:S(2)}) collective-permute-start(s16[1088,256]{1,0:T(8,128)(2,1)} %get-tuple-element.119), channel_id=1, source_target_pairs={{0,1},{1,0},{2,3},{3,2},{4,5},{5,4},{6,7},{7,6},{8,9},{9,8},{10,11... | collective-permute-start | bytes 1671176 | tf_op jit(solution)/shard_map/ppermute | solution.py:1134
  166.5 16.2 %all-to-all-start.2 = ((f32[128,1,128]{2,1,0:T(1,128)}), f32[128,1,128]{2,1,0:T(1,128)S(1)}, u32[]{:S(2)}, u32[]{:S(2)}) async-start(f32[128,1,128]{2,1,0:T(1,128)} %get-tuple-element.117), calls=%async_computation.2 | async-start | bytes 131072 | tf_op jit(solution)/shard_map/all_to_all | solution.py:1136
  (7 other events, 22.2 us)
